TPU v7x, 32 devices: a whole 2x2x4 slice. The times are simulated.
32 devices in a mesh: groups: 2 (over y), row: 4 (over z), col: 2 (over x), sub: 2 (over core).
Axes of the slice: x: 2, y: 2, z: 4, core: 2. Of those that a mesh axis runs over, the one named last changes fastest.
Arguments:
- density: bfloat16 [4096, 2048], P(('groups', 'row'), ('col', 'sub')), parts along dimension 0, as said below
- margin: bfloat16 [4096, 2048], P(('groups', 'row'), ('col', 'sub')), parts along dimension 0, as said below
- pattern_d: int32 [32, 16], P(('groups', 'row'), ('col', 'sub')), parts along dimension 0, may hold values from 0 to 1, as said below
- pattern_s: int32 [32, 16], P(('groups', 'row'), ('col', 'sub')), parts along dimension 0, may hold values from 0 to 1, as said below
- dipole: bfloat16 [3, 4096], P(None, ('groups', 'col', 'sub')), parts along dimension 1, may hold values from -0.125 to 0.125
- owner: int32 [3, 32768], P(None, ('groups', 'row', 'col', 'sub')), parts along dimension 1, may hold values from 0 to 2047
- centres: float32 [3, 32768], P(None, ('groups', 'row', 'col', 'sub')), parts along dimension 1, may hold values from 0 to 3
- angles: float32 [3, 32768], P(None, ('groups', 'row', 'col', 'sub')), parts along dimension 1, may hold values from -3.140625 to 3.140625
- velocity: float32 [3, 32768], P(None, ('groups', 'row', 'col', 'sub')), parts along dimension 1, may hold values from -6 to 6
- angmom: float32 [3, 32768], P(None, ('groups', 'row', 'col', 'sub')), parts along dimension 1, may hold values from -6 to 6
- halo_list: int32 [2, 8192], P(None, ('groups', 'row', 'col', 'sub')), parts along dimension 1, may hold values from 0 to 1023
- neighbours: int32 [32, 32768], P(None, ('groups', 'row', 'col', 'sub')), parts along dimension 1, may hold values from 0 to 1535
Outputs:
- qm_out: bfloat16 [4096, 2048], P(('groups', 'row'), ('col', 'sub')), parts along dimension 0
- centres_new: float32 [3, 32768], P(None, ('groups', 'row', 'col', 'sub')), parts along dimension 1
- velocity_new: float32 [3, 32768], P(None, ('groups', 'row', 'col', 'sub')), parts along dimension 1
- angmom_new: float32 [3, 32768], P(None, ('groups', 'row', 'col', 'sub')), parts along dimension 1
- orient_new: float32 [4, 32768], P(None, ('groups', 'row', 'col', 'sub')), parts along dimension 1
There are 2 independent parts, one for each index of `groups`. A program takes and returns all parts, laid end to end along the dimension named above; each array names one. Nothing has to cross between parts.
Inputs may be any that keep to these rules, and one draw needn't show every extreme that they name: density is symmetric. margin is symmetric. `pattern_d`: symmetric, ones on the diagonal. `pattern_s`: every block row holds exactly 1 ones in each aligned run of 4 block columns.
All inputs are finite; a program needn't handle non-finite values.
Results may differ from a plain program's by a relative error of at most 0.0075.
Values may be sent and summed in bfloat16 or wider, within the bound.
No kernel may reach another device: no remote copies, remote signals or barrier semaphores. Data moves between devices by JAX's collectives and lax.ppermute only.
A program may use at most 128 MiB of HBM per device.

v0:
```python
import jax
import jax.numpy as jnp
from jax import lax
from jax.sharding import PartitionSpec as P

BLOCK = 128


CHARGE = (-0.834, 0.417, 0.417)
OFFSET = ((0.0, 0.0, -0.12), (0.76, 0.0, 0.47), (-0.76, 0.0, 0.47))
COUPLE = 0.1
STEP_DT = 0.5
WATER_MASS = 1.0
INERTIA = 0.5
SOFTEN = 1.0


def from_behind(value, axis, by):
    length = lax.axis_size(axis)
    return lax.ppermute(value, axis, [(i, (i + by) % length) for i in range(length)])


def expand(pattern, width):
    return jnp.repeat(jnp.repeat(pattern, width, axis=0), width, axis=1)


def quaternion(angles):
    half_angle = 0.5 * angles
    cos_r, cos_p, cos_y = (jnp.cos(half_angle[0]), jnp.cos(half_angle[1]), jnp.cos(half_angle[2]))
    sin_r, sin_p, sin_y = (jnp.sin(half_angle[0]), jnp.sin(half_angle[1]), jnp.sin(half_angle[2]))
    comp_w = cos_r * cos_p * cos_y + sin_r * sin_p * sin_y
    comp_x = sin_r * cos_p * cos_y - cos_r * sin_p * sin_y
    comp_y = cos_r * sin_p * cos_y + sin_r * cos_p * sin_y
    comp_z = cos_r * cos_p * sin_y - sin_r * sin_p * cos_y
    return jnp.stack([comp_w, comp_x, comp_y, comp_z])


def rotation(quat):
    comp_w, comp_x, comp_y, comp_z = (quat[0], quat[1], quat[2], quat[3])
    return (
        (
            1.0 - 2.0 * (comp_y * comp_y + comp_z * comp_z),
            2.0 * (comp_x * comp_y - comp_w * comp_z),
            2.0 * (comp_x * comp_z + comp_w * comp_y),
        ),
        (
            2.0 * (comp_x * comp_y + comp_w * comp_z),
            1.0 - 2.0 * (comp_x * comp_x + comp_z * comp_z),
            2.0 * (comp_y * comp_z - comp_w * comp_x),
        ),
        (
            2.0 * (comp_x * comp_z - comp_w * comp_y),
            2.0 * (comp_y * comp_z + comp_w * comp_x),
            1.0 - 2.0 * (comp_x * comp_x + comp_y * comp_y),
        ),
    )


def site_positions(centres, quat):
    matrix = rotation(quat)
    layers = []
    for source in range(3):
        for compo in range(3):
            layers.append(
                centres[compo]
                + matrix[compo][0] * OFFSET[source][0]
                + matrix[compo][1] * OFFSET[source][1]
                + matrix[compo][2] * OFFSET[source][2]
            )
    return jnp.stack(layers)


def pair_forces(own_sites, partner_sites):
    pieces = []
    for source in range(3):
        own_part = own_sites[3 * source : 3 * source + 3][:, None]
        total = jnp.zeros((3,) + own_sites.shape[1:], jnp.float32)
        for target in range(3):
            offset_vec = own_part - partner_sites[3 * target : 3 * target + 3]
            dist_sq = jnp.sum(offset_vec * offset_vec, axis=0) + SOFTEN
            weight = CHARGE[source] * CHARGE[target] * dist_sq ** (-1.5)
            total = total + jnp.sum(offset_vec * weight[None], axis=1)
        pieces.append(total)
    return jnp.concatenate(pieces, axis=0)


def advance(centres, quat, velocity, angmom, sites, forces):
    total = forces[0:3] + forces[3:6] + forces[6:9]
    torque = jnp.zeros_like(centres)
    for source in range(3):
        lever = sites[3 * source : 3 * source + 3] - centres
        torque = torque + jnp.cross(lever, forces[3 * source : 3 * source + 3], axis=0)
    velocity_new = velocity + STEP_DT * total / WATER_MASS
    centres_new = centres + STEP_DT * velocity_new
    angmom_new = angmom + STEP_DT * torque
    omega = angmom_new / INERTIA
    vector = quat[1:4]
    delta_w = -jnp.sum(omega * vector, axis=0)
    delta_vec = quat[0][None] * omega + jnp.cross(omega, vector, axis=0)
    moved = quat + 0.5 * STEP_DT * jnp.concatenate([delta_w[None], delta_vec], axis=0)
    length = jnp.sqrt(jnp.sum(moved * moved, axis=0))
    return (centres_new, velocity_new, angmom_new, moved / length[None])


def pass_halo(values, steps):
    return from_behind(values, "row", steps)


def shards(
    density,
    margin,
    pattern_d,
    pattern_s,
    dipole,
    owner,
    centres,
    angles,
    velocity,
    angmom,
    halo_list,
    neighbours,
):
    dens_mask = density * expand(pattern_d, BLOCK).astype(jnp.bfloat16)
    over_mask = margin * expand(pattern_s, BLOCK).astype(jnp.bfloat16)
    rows_loc, cols_loc = dens_mask.shape
    order_all = rows_loc * lax.axis_size("row")
    row_start = lax.axis_index("row") * rows_loc
    col_start = lax.axis_index(("col", "sub")) * cols_loc
    site_charge = jnp.broadcast_to(jnp.array(CHARGE, jnp.float32)[:, None], owner.shape)
    local_charge = jax.ops.segment_sum(
        site_charge.reshape(-1), owner.reshape(-1), num_segments=order_all
    )
    potential = lax.psum(local_charge, ("row", "col", "sub"))
    panel = lax.all_gather(dens_mask, ("col", "sub"), axis=1, tiled=True)
    product = jnp.dot(
        panel,
        lax.all_gather(over_mask, "row", axis=0, tiled=True),
        preferred_element_type=jnp.float32,
    )
    row_pot = lax.dynamic_slice_in_dim(potential, row_start, rows_loc)
    col_pot = lax.dynamic_slice_in_dim(potential, col_start, cols_loc)
    qm_out = (
        product + COUPLE * (row_pot[:, None] + col_pot[None, :]) * dens_mask.astype(jnp.float32)
    ).astype(jnp.bfloat16)
    field_part = lax.dot_general(
        dipole, qm_out, (((1,), (1,)), ((), ())), preferred_element_type=jnp.float32
    )
    spread_out = lax.dynamic_update_slice_in_dim(
        jnp.zeros((3, order_all), jnp.float32), field_part, row_start, 1
    )
    qm_field = lax.psum(spread_out, ("row", "col", "sub"))
    quat = quaternion(angles)
    sites = site_positions(centres, quat)
    send_up = sites[:, halo_list[0]]
    send_down = sites[:, halo_list[1]]
    from_below = pass_halo(send_up, 1)
    from_above = pass_halo(send_down, -1)
    table = jnp.concatenate([sites, from_below, from_above], axis=1)
    partner = table[:, neighbours]
    forces = pair_forces(sites, partner)
    field_parts = []
    for source in range(3):
        field_parts.append(
            forces[3 * source : 3 * source + 3]
            + CHARGE[source] * jnp.take(qm_field, owner[source], axis=1)
        )
    forces = jnp.concatenate(field_parts, axis=0)
    centres_new, velocity_new, angmom_new, orient_new = advance(
        centres, quat, velocity, angmom, sites, forces
    )
    return (qm_out, centres_new, velocity_new, angmom_new, orient_new)


def solution(mesh):
    return jax.shard_map(
        shards,
        mesh=mesh,
        in_specs=(
            P(("groups", "row"), ("col", "sub")),
            P(("groups", "row"), ("col", "sub")),
            P(("groups", "row"), ("col", "sub")),
            P(("groups", "row"), ("col", "sub")),
            P(None, ("groups", "col", "sub")),
            P(None, ("groups", "row", "col", "sub")),
            P(None, ("groups", "row", "col", "sub")),
            P(None, ("groups", "row", "col", "sub")),
            P(None, ("groups", "row", "col", "sub")),
            P(None, ("groups", "row", "col", "sub")),
            P(None, ("groups", "row", "col", "sub")),
            P(None, ("groups", "row", "col", "sub")),
        ),
        out_specs=(
            P(("groups", "row"), ("col", "sub")),
            P(None, ("groups", "row", "col", "sub")),
            P(None, ("groups", "row", "col", "sub")),
            P(None, ("groups", "row", "col", "sub")),
            P(None, ("groups", "row", "col", "sub")),
        ),
        check_vma=False,
    )
```

profile of v0, /device:TPU:0, one launch (start us, length us, event | category | flops | bytes accessed | tf_op | source)
XLA Modules:
  0.0 416.6 jit_solution(11929673567620565862)
XLA Ops:
  7.2 0.7 convert_element_type.28
  7.9 0.6 broadcast_in_dim.23
  8.5 1.9 bitcast_multiply_fusion.1
  10.5 0.7 broadcast_multiply_fusion
  11.3 0.4 broadcast_multiply_fusion.1
  11.6 1.1 add_add_fusion
  12.7 0.9 add_add_fusion.3
  13.6 0.8 add_add_fusion.4
  14.5 0.1 stack.13
  14.6 0.2 copy.302
  14.8 0.8 compare_select_fusion.5
  15.6 0.7 gather_fusion
  16.3 0.1 copy.303
  16.4 3.0 collective-permute-start
  19.4 0.7 gather_fusion.1
  20.1 0.1 copy.305
  20.2 2.1 collective-permute-start.1
  22.3 0.7 convert_element_type.31
  23.0 0.6 broadcast_in_dim.25
  23.6 1.9 bitcast_multiply_fusion
  25.5 0.8 subtract_bitcast_fusion.2
  26.3 0.7 reshape.317
  27.0 0.8 fusion.22
  28.0 0.9 fusion.1
  29.0 0.7 broadcast_in_dim.27
  29.7 16.7 %scatter_custom_fusion = f32[2048]{0:T(1024)S(1)} fusion(s32[3072]{0:T(1024)S(1)} %reshape.317, f32[3072]{0:T(1024)S(1)} %reshape.319, f32[]{:T(128)} %constant.38.clone.1), kind=kCustom, calls=%fused_computation.108 | custom fusion | flops 3072 | bytes 8196 | tf_op jit(solution)/shard_map/scatter-add | solution.py:130
  46.4 33.6 %psum.14 = f32[2048]{0:T(1024)S(1)} all-reduce(f32[2048]{0:T(1024)S(1)} %scatter_custom_fusion), channel_id=1, replica_groups=mesh['groups'=2,'row'=4,'col'=2,'sub'=2] {'row','col','sub'}, use_global_device_ids=true, to_apply=%region_1.0 | all-reduce | flops 2048 | bytes 16384 | tf_op jit(solution)/shard_map/psum | solution.py:133
  80.0 0.1 fusion.23
  80.1 0.2 copy.301
  80.3 0.2 copy.312
  80.6 0.2 copy.317
  80.9 0.3 copy.306
  81.1 108.2 %gather_fusion.2 = f32[32768,9]{1,0:T(8,128)} fusion(f32[9,1536]{0,1:T(8,128)S(1)} %copy.306, s32[32768]{0:T(1024)S(1)} %broadcast_clamp_fusion), kind=kCustom, calls=%fused_computation.5 | custom fusion | bytes 2490368 | tf_op jit(solution)/shard_map/gather | solution.py:159
  189.4 35.6 %multiply_reduce_fusion.9 = (f32[32,1024]{1,0:T(8,128)S(1)}, f32[32,1024]{1,0:T(8,128)S(1)}, f32[32,1024]{1,0:T(8,128)S(1)}, f32[32,1024]{1,0:T(8,128)S(1)}, f32[32,1024]{1,0:T(8,128)S(1)}) fusion(f32[9,32,1024]{0,2,1:T(8,128)} %bitcast.85, f32[3,1024]{0,1:T(8,128)S(1)} %copy.312, f32[3,1024]{0,1:T(8,128)S(1)} %copy.317, f32[3,1024]{0,1:T(8,128)S(1)} %copy.301), kind=kLoop, calls=%fused_computation.16 | loop fusion | flops 1310720 | bytes 1871872 | tf_op jit(solution)/shard_map/reduce_sum | solution.py:80
  225.0 0.1 power_multiply_fusion.1
  225.1 26.0 %multiply_reduce_fusion.2 = (f32[3,1024]{0,1:T(8,128)S(1)}, f32[32,1024]{1,0:T(8,128)S(1)}, f32[32,1024]{1,0:T(8,128)S(1)}) fusion(f32[9,32,1024]{0,2,1:T(8,128)} %bitcast.86, f32[32,1024]{1,0:T(8,128)S(1)} %get-tuple-element.124, f32[3,1024]{0,1:T(8,128)S(1)} %copy.317), kind=kLoop, calls=%fused_computation.9 | loop fusion | flops 816128 | bytes 1597440 | tf_op jit(solution)/shard_map/reduce_sum | solution.py:82
  251.1 0.1 power_multiply_fusion
  251.1 0.1 power_multiply_fusion.2
  251.3 0.1 power_multiply_fusion.6
  251.4 50.8 %multiply_reduce_fusion.8 = (f32[3,1024]{0,1:T(8,128)}, f32[32,1024]{1,0:T(8,128)S(1)}, f32[32,1024]{1,0:T(8,128)S(1)}, f32[3,1024]{0,1:T(8,128)S(1)}, f32[3,102...) fusion(f32[9,32,1024]{0,2,1:T(8,128)} %bitcast.87, ...), kind=kLoop, calls=%fused_computation.15 | loop fusion | flops 2275328 | bytes 2338816 | tf_op jit(solution)/shard_map/reduce_sum | solution.py:82
  302.4 17.4 %multiply_reduce_fusion.10 = (f32[3,1024]{0,1:T(8,128)}, f32[3,1024]{0,1:T(8,128)}) fusion(f32[9,32,1024]{0,2,1:T(8,128)} %bitcast.88, f32[32,1024]{1,0:T(8,128)S(1)} %power_multiply_fusion.5, f32[3,1024]{0,1:T(8,128)S(1)} %copy.312, f32[32,1024]{1,0:T(8,128)S(1)} %power_multiply_fusion.3), kind=kLoop, calls=%fused_computation.17 | loop fusion | flops 583680 | bytes 1085440 | tf_op jit(solution)/shard_map/reduce_sum | solution.py:82
  319.8 1.2 copy.313
  321.0 1.2 copy.315
  322.3 1.2 copy.307
  323.5 1.2 copy.308
  324.7 0.2 copy.309
  324.9 0.2 copy.314
  325.1 0.2 copy.318
  325.3 0.2 copy.320
  325.5 0.2 copy.319
  325.8 3.6 fusion
  329.3 0.2 convolution_bitcast_fusion
  329.6 0.2 copy.310
  329.7 0.1 broadcast_in_dim.29
  329.9 69.2 %psum.15 = f32[3,2048]{0,1:T(8,128)S(1)} all-reduce(f32[3,2048]{0,1:T(8,128)S(1)} %constant_dynamic-update-slice_fusion), channel_id=1, replica_groups=mesh['groups'=2,'row'=4,'col'=2,'sub'=2] {'row','col','sub'}, use_global_device_ids=true, to_apply=%region_8.0 | all-reduce | flops 6144 | bytes 49152 | tf_op jit(solution)/shard_map/psum | solution.py:151
  399.1 2.8 gather_fusion.3
  401.9 0.2 copy.311
  402.1 2.8 gather_fusion.4
  404.9 0.2 copy.316
  405.1 2.8 gather_fusion.5
  407.9 0.2 copy.321
  408.1 0.7 multiply_add_fusion
  408.9 0.1 multiply_reduce_fusion.19
  409.1 0.6 broadcast_divide_fusion
  (50 shorter events, 0.7 us)
Async XLA Ops:
  7.2 322.2 %copy-start = (bf16[3,512]{1,0:T(4,128)(2,1)S(1)}, bf16[3,512]{1,0:T(4,128)(2,1)}, u32[]{:S(2)}) copy-start(bf16[3,512]{1,0:T(4,128)(2,1)} %param.21) | copy-start | bytes 9220
  7.2 318.6 %all-gather.3.cloned.1.call-start = ((), (), s32[]{:S(2)}) async-start(), calls=%async_computation | async-start | bytes 2621440 | tf_op jit(solution)/shard_map/all_gather | solution.py:134
  10.5 315.3 %all-gather.5.cloned.1.call-start = ((), (), s32[]{:S(2)}) async-start(), calls=%async_computation.1 | async-start | bytes 2621440 | tf_op jit(solution)/shard_map/all_gather | solution.py:137
  16.4 64.5 %collective-permute-start = (f32[9,256]{1,0:T(8,128)S(1)}, f32[9,256]{1,0:T(8,128)S(1)}, u32[]{:S(2)}, u32[]{:S(2)}) collective-permute-start(f32[9,256]{1,0:T(8,128)S(1)} %bitcast.104), channel_id=1, source_target_pairs={{0,4},{4,8},{8,12},{12,0},{1,5},{5,9},{9,13},{13,1},{2,6},{6,10},{... | collective-permute-start | bytes 27656 | tf_op jit(solution)/shard_map/ppermute | solution.py:20
  20.2 60.6 %collective-permute-start.1 = (f32[9,256]{1,0:T(8,128)S(1)}, f32[9,256]{1,0:T(8,128)S(1)}, u32[]{:S(2)}, u32[]{:S(2)}) collective-permute-start(f32[9,256]{1,0:T(8,128)S(1)} %bitcast.105), channel_id=1, source_target_pairs={{0,12},{4,0},{8,4},{12,8},{1,13},{5,1},{9,5},{13,9},{2,14},{6,2},{... | collective-permute-start | bytes 27656 | tf_op jit(solution)/shard_map/ppermute | solution.py:20
  302.3 22.4 %copy-start.2 = (f32[3,1024]{0,1:T(8,128)S(1)}, f32[3,1024]{0,1:T(8,128)}, u32[]{:S(2)}) copy-start(f32[3,1024]{0,1:T(8,128)} %get-tuple-element.50) | copy-start | bytes 36868
  302.3 22.6 %copy-start.1 = (f32[3,1024]{0,1:T(8,128)S(1)}, f32[3,1024]{0,1:T(8,128)}, u32[]{:S(2)}) copy-start(f32[3,1024]{0,1:T(8,128)} %get-tuple-element.32) | copy-start | bytes 36868
  319.8 88.4 %copy-start.4 = (f32[3,1024]{1,0:T(4,128)S(1)}, f32[3,1024]{1,0:T(4,128)}, u32[]{:S(2)}) copy-start(f32[3,1024]{1,0:T(4,128)} %param.23) | copy-start | bytes 36868
  319.8 88.4 %copy-start.6 = (f32[3,1024]{1,0:T(4,128)S(1)}, f32[3,1024]{1,0:T(4,128)}, u32[]{:S(2)}) copy-start(f32[3,1024]{1,0:T(4,128)} %param.25) | copy-start | bytes 36868
  319.8 89.1 %copy-start.7 = (f32[3,1024]{1,0:T(4,128)S(1)}, f32[3,1024]{1,0:T(4,128)}, u32[]{:S(2)}) copy-start(f32[3,1024]{1,0:T(4,128)} %param.26) | copy-start | bytes 36868
  329.3 80.4 %copy-start.3 = (bf16[512,512]{1,0:T(8,128)(2,1)}, bf16[512,512]{1,0:T(8,128)(2,1)S(1)}, u32[]{:S(2)}) copy-start(bf16[512,512]{1,0:T(8,128)(2,1)S(1)} %fusion) | copy-start | bytes 1572868
  409.0 0.8 copy-start.5
Sparse Core Ops, SparseCore 0:
  10.6 25.2 all-gather.2
  37.5 46.4 all-gather.4
where the time goes:
time: 418 us; the launch traced here: 417 us
  other arithmetic  160 us (38%)
  local copies, waits for them, and re-layouts  130 us (31%)
  blocking collectives  103 us (25%)
  between operations  14.5 us (3%)
  starting transfers between devices  5.18 us (1%)
    gather x1, local copies, waits for them, and re-layouts, shards(): partner = table[:, neighbours]  108 us
    reduce_sum x3, other arithmetic, pair_forces(): total = total + jnp.sum(offset_vec * weight[None], axis=1)  94.2 us
    psum x1, blocking collectives, shards(): qm_field = lax.psum(spread_out, ('row', 'col', 'sub'))  69.2 us
    reduce_sum x1, other arithmetic, pair_forces(): dist_sq = jnp.sum(offset_vec * offset_vec, axis=0) + SOFTEN  35.6 us
    psum x1, blocking collectives, shards(): potential = lax.psum(local_charge, ('row', 'col', 'sub'))  33.6 us
    scatter-add x1, other arithmetic, shards(): jax.ops.segment_sum(site_charge.reshape(-1), owner.reshape(-1), num_segme...  16.7 us
    gather x6, local copies, waits for them, and re-layouts, shards(): jnp.take(qm_field, owner[source], axis=1)  9 us
  transfers between devices with their start and end apart: 4, of which 0 were waited for; matrix products, arithmetic and copies ran while one was open for 66% of the time, Pallas kernels for 0%

commit v1 on v0

v1 whole, which is shorter than its diff:
```python
import functools

import jax
import jax.numpy as jnp
from jax import lax
from jax.experimental import pallas as pl
from jax.experimental.pallas import tpu as pltpu
from jax.sharding import PartitionSpec as P

BLOCK = 128
LANES = 128

CHARGE = (-0.834, 0.417, 0.417)
UNIT = 0.417
MULTIPLE = (-2.0, 1.0, 1.0)
OFFSET = ((0.0, 0.0, -0.12), (0.76, 0.0, 0.47), (-0.76, 0.0, 0.47))
COUPLE = 0.1
STEP_DT = 0.5
WATER_MASS = 1.0
INERTIA = 0.5
SOFTEN = 1.0

F32 = jnp.float32
BF16 = jnp.bfloat16

SIN_TERMS = (-1 / 6, 1 / 120, -1 / 5040, 1 / 362880, -1 / 39916800, 1 / 6227020800)
COS_TERMS = (-1 / 2, 1 / 24, -1 / 720, 1 / 40320, -1 / 3628800, 1 / 479001600, -1 / 87178291200)


def at(tile):
    return slice(tile * LANES, (tile + 1) * LANES)


def pick(table, index):
    return jnp.take_along_axis(table, index, axis=1, mode="promise_in_bounds")


def contract(left, right, dims):
    return lax.dot_general(left, right, (dims, ((), ())), preferred_element_type=F32)


def series(square, terms):
    total = jnp.full_like(square, terms[-1])
    for term in terms[-2::-1]:
        total = total * square + term
    return total * square + 1.0


def open_kernel(pat_d, pat_s, marg, dip, owner, small, message, expanded):
    rows_b, cols_b = pat_d.shape
    hist_rows = message.shape[0] - 8 * max(rows_b, cols_b) - rows_b * cols_b
    message[...] = jnp.zeros(message.shape, F32)
    pattern_at = hist_rows + 8 * max(rows_b, cols_b)
    for row in range(rows_b):
        chosen = jnp.int32(0)
        for col in range(cols_b):
            chosen = chosen + col * pat_s[row, col]
            line = row * cols_b + col
            expanded[line : line + 1, :] = jnp.full((1, LANES), pat_s[row, col].astype(F32))
            message[pattern_at + line : pattern_at + line + 1, :] = jnp.full((1, LANES), pat_d[row, col].astype(F32))
        span = pl.ds(pl.multiple_of(chosen * BLOCK, BLOCK), BLOCK)
        block = marg[row * BLOCK : (row + 1) * BLOCK, span]
        small[row * BLOCK : (row + 1) * BLOCK, :] = block
        start = hist_rows + 8 * row
        message[start : start + 3, :] = contract(dip[:, span], block, ((1,), (1,)))
    for col in range(cols_b):
        start = hist_rows + 8 * col + 3
        message[start : start + 3, :] = dip[:, at(col)].astype(F32)
    waters = owner.shape[1]
    count = jnp.zeros((hist_rows, LANES), F32)
    for source in range(3):
        line = owner[source : source + 1, :]
        high = lax.broadcasted_iota(jnp.int32, (hist_rows, waters), 0) == (line >> 7)
        low = lax.broadcasted_iota(jnp.int32, (LANES, waters), 0) == (line & 127)
        count = count + contract(
            jnp.where(high, MULTIPLE[source], 0.0).astype(BF16),
            jnp.where(low, 1.0, 0.0).astype(BF16),
            ((1,), (1,)),
        )
    message[0:hist_rows, :] = count


def gathered_kernel(ways, hist_rows, *refs):
    messages, expanded, out = refs[:ways], refs[ways], refs[ways + 1]
    total = messages[0][0:hist_rows, :]
    for other in messages[1:]:
        total = total + other[0:hist_rows, :]
    out[0:hist_rows, :] = total
    out[hist_rows:, :] = expanded[...]


def project_kernel(ways, rows_n, hist_rows, where, pat_d, dens, *refs):
    firsts, seconds = refs[:ways], refs[ways : ways + rows_n]
    pot, out, dips, lines, masked = refs[ways + rows_n :]
    rows_b, cols_b = pat_d.shape
    here_row, here_col = where[0], where[1]
    total = seconds[0][0:hist_rows, :]
    for other in seconds[1:]:
        total = total + other[0:hist_rows, :]
    pot[...] = UNIT * total
    depth = 8 * max(rows_b, cols_b)
    for step in range(ways):
        dips[here_col ^ step] = firsts[step][hist_rows : hist_rows + depth, :]
    for row in range(rows_b):
        place = here_row * rows_b + row
        device = place // cols_b
        tile = dips[device, pl.ds(pl.multiple_of(8 * (place % cols_b), 8), 8), :]
        summed = firsts[0][hist_rows + 8 * row : hist_rows + 8 * row + 3, :]
        for other in firsts[1:]:
            summed = summed + other[hist_rows + 8 * row : hist_rows + 8 * row + 3, :]
        dip = tile[3:6, :]
        lines[0:3, at(row)] = summed + COUPLE * pot[pl.ds(place, 1), :] * dip
        lines[3:6, at(row)] = dip
        lines[6:8, at(row)] = jnp.zeros((2, LANES), F32)
        for col in range(cols_b):
            block = dens[row * BLOCK : (row + 1) * BLOCK, at(col)]
            masked[row * BLOCK : (row + 1) * BLOCK, at(col)] = jnp.where(
                pat_d[row, col] != 0, block, jnp.zeros_like(block)
            )
    whole = lines[...]
    first = whole.astype(BF16)
    second = (whole - first.astype(F32)).astype(BF16)
    out[...] = contract(first, masked[...], ((1,), (0,))) + contract(second, masked[...], ((1,), (0,)))


def field_kernel(rows_n, where, pot, *refs):
    parts, out = refs[:rows_n], refs[rows_n]
    cols_b = out.shape[1] // BLOCK
    total = parts[0][...]
    for other in parts[1:]:
        total = total + other[...]
    out[...] = jnp.zeros(out.shape, F32)
    for col in range(cols_b):
        line = pot[pl.ds(where[1] * cols_b + col, 1), :]
        out[0:3, at(col)] = total[0:3, at(col)] + COUPLE * line * total[3:6, at(col)]


def sites_kernel(centres, angles, halo, sites, quat, up, down):
    half_angle = 0.5 * angles[...]
    square = half_angle * half_angle
    sine = half_angle * series(square, SIN_TERMS)
    cosine = series(square, COS_TERMS)
    sin_r, sin_p, sin_y = sine[0:1], sine[1:2], sine[2:3]
    cos_r, cos_p, cos_y = cosine[0:1], cosine[1:2], cosine[2:3]
    comp_w = cos_r * cos_p * cos_y + sin_r * sin_p * sin_y
    comp_x = sin_r * cos_p * cos_y - cos_r * sin_p * sin_y
    comp_y = cos_r * sin_p * cos_y + sin_r * cos_p * sin_y
    comp_z = cos_r * cos_p * sin_y - sin_r * sin_p * cos_y
    for place, comp in enumerate((comp_w, comp_x, comp_y, comp_z)):
        quat[place : place + 1, :] = comp
    first = (
        1.0 - 2.0 * (comp_y * comp_y + comp_z * comp_z),
        2.0 * (comp_x * comp_y + comp_w * comp_z),
        2.0 * (comp_x * comp_z - comp_w * comp_y),
    )
    third = (
        2.0 * (comp_x * comp_z + comp_w * comp_y),
        2.0 * (comp_y * comp_z - comp_w * comp_x),
        1.0 - 2.0 * (comp_x * comp_x + comp_y * comp_y),
    )
    sites[...] = jnp.zeros(sites.shape, F32)
    for source in range(3):
        for compo in range(3):
            place = 3 * source + compo
            position = centres[compo : compo + 1, :] + third[compo] * OFFSET[source][2]
            if OFFSET[source][0] != 0.0:
                position = position + first[compo] * OFFSET[source][0]
            sites[place : place + 1, :] = position
    waters, listed = centres.shape[1], halo.shape[1]
    for which, out in enumerate((up, down)):
        for tile in range(listed // LANES):
            index = jnp.broadcast_to(halo[which : which + 1, at(tile)], (8, LANES))
            low, high = index & 127, index >> 7
            for part in range(2):
                found = jnp.zeros((8, LANES), F32)
                for source in range(waters // LANES):
                    value = pick(sites[8 * part : 8 * part + 8, at(source)], low)
                    found = jnp.where(high == source, value, found)
                out[8 * part : 8 * part + 8, at(tile)] = found


def pair_kernel(sites, below, above, neighbours, force, table):
    waters, listed, slots = sites.shape[1], below.shape[1], neighbours.shape[0]
    own_tiles, halo_tiles = waters // LANES, listed // LANES
    tiles = own_tiles + 2 * halo_tiles
    for word in range(9):
        for tile in range(tiles):
            if tile < own_tiles:
                line = sites[word : word + 1, at(tile)]
            elif tile < own_tiles + halo_tiles:
                line = below[word : word + 1, at(tile - own_tiles)]
            else:
                line = above[word : word + 1, at(tile - own_tiles - halo_tiles)]
            table[word, tile] = jnp.broadcast_to(line, (8, LANES))

    def one_tile(tile, carry):
        span = pl.ds(pl.multiple_of(tile * LANES, LANES), LANES)
        near = [jnp.zeros((8, LANES), F32) for _ in range(9)]
        far = [jnp.zeros((8, LANES), F32) for _ in range(9)]
        for pair in range(slots // 16):
            index = [neighbours[16 * pair + 8 * part : 16 * pair + 8 * part + 8, span] for part in range(2)]
            low = [value & 127 for value in index]
            high = [value >> 7 for value in index]
            found = [[None, None] for _ in range(9)]
            for source in range(tiles):
                here = [value == source for value in high]
                for word in range(9):
                    line = table[word, source]
                    for part in range(2):
                        value = pick(line, low[part])
                        found[word][part] = (
                            value if source == 0 else jnp.where(here[part], value, found[word][part])
                        )
            for part in range(2):
                for source in range(3):
                    own = [table[3 * source + compo, tile] for compo in range(3)]
                    for target in range(3):
                        gap = [own[compo] - found[3 * target + compo][part] for compo in range(3)]
                        root = lax.rsqrt(gap[0] * gap[0] + gap[1] * gap[1] + gap[2] * gap[2] + SOFTEN)
                        weight = root * root * root
                        sums = near if target == 0 else far
                        for compo in range(3):
                            sums[3 * source + compo] = sums[3 * source + compo] + gap[compo] * weight
        for place in range(9):
            factor = CHARGE[place // 3] * UNIT
            total = factor * (far[place] - 2.0 * near[place])
            force[place : place + 1, span] = jnp.sum(total, axis=0, keepdims=True)
        return carry

    lax.fori_loop(0, own_tiles, one_tile, 0)


def advance_kernel(ways, where, owner, sites, quat, pair, centres, velocity, angmom, *refs):
    fields = refs[:ways]
    centres_new, velocity_new, angmom_new, orient_new, force = refs[ways:]
    waters = owner.shape[1]
    cols_b = fields[0].shape[1] // BLOCK
    for tile in range(waters // LANES):
        for source in range(3):
            index = jnp.broadcast_to(owner[source : source + 1, at(tile)], (8, LANES))
            low, high = index & 127, index >> 7
            found = jnp.zeros((8, LANES), F32)
            for step in range(ways):
                base = (where[1] ^ step) * cols_b
                for col in range(cols_b):
                    value = pick(fields[step][:, at(col)], low)
                    found = jnp.where(high == base + col, value, found)
            lines = slice(3 * source, 3 * source + 3)
            force[lines, at(tile)] = pair[lines, at(tile)] + CHARGE[source] * found[0:3]

    def cross(left, right):
        return [
            left[1] * right[2] - left[2] * right[1],
            left[2] * right[0] - left[0] * right[2],
            left[0] * right[1] - left[1] * right[0],
        ]

    def split(array):
        return [array[compo : compo + 1, :] for compo in range(3)]

    total = force[0:3, :] + force[3:6, :] + force[6:9, :]
    torque = None
    centre = split(centres)
    for source in range(3):
        lever = [sites[3 * source + compo : 3 * source + compo + 1, :] - centre[compo] for compo in range(3)]
        push = [force[3 * source + compo : 3 * source + compo + 1, :] for compo in range(3)]
        turn = cross(lever, push)
        torque = turn if torque is None else [old + new for old, new in zip(torque, turn)]
    moving = velocity[...] + STEP_DT * total / WATER_MASS
    velocity_new[...] = moving
    centres_new[...] = centres[...] + STEP_DT * moving
    spin = [angmom[compo : compo + 1, :] + STEP_DT * torque[compo] for compo in range(3)]
    for compo in range(3):
        angmom_new[compo : compo + 1, :] = spin[compo]
    omega = [value * (1.0 / INERTIA) for value in spin]
    scalar = quat[0:1, :]
    vector = [quat[compo + 1 : compo + 2, :] for compo in range(3)]
    delta = [-(omega[0] * vector[0] + omega[1] * vector[1] + omega[2] * vector[2])]
    turned = cross(omega, vector)
    delta = delta + [scalar * omega[compo] + turned[compo] for compo in range(3)]
    moved = [old + 0.5 * STEP_DT * new for old, new in zip([scalar] + vector, delta)]
    length = jnp.sqrt(moved[0] * moved[0] + moved[1] * moved[1] + moved[2] * moved[2] + moved[3] * moved[3])
    for place in range(4):
        orient_new[place : place + 1, :] = moved[place] / length


def product_kernel(ways, rows_n, hist_rows, where, pot, *refs):
    firsts, seconds = refs[:ways], refs[ways : ways + rows_n]
    refs = refs[ways + rows_n :]
    dens, small = refs[:ways], refs[ways : ways + rows_n]
    out, panel, masked, total = refs[ways + rows_n :]
    rows, cols = out.shape
    rows_b, cols_b = rows // BLOCK, cols // BLOCK
    here_row, here_col = where[0], where[1]
    for step in range(rows_n):
        base = (here_row ^ step) * rows
        for row in range(rows_b):
            block = small[step][row * BLOCK : (row + 1) * BLOCK, :]
            for col in range(cols_b):
                line = hist_rows + row * cols_b + col
                keep = seconds[step][line : line + 1, :].astype(BF16)
                start = pl.multiple_of(base + row * BLOCK, BLOCK)
                panel[pl.ds(start, BLOCK), at(col)] = block * keep
    pattern_at = hist_rows + 8 * max(rows_b, cols_b)
    lane = lax.broadcasted_iota(jnp.int32, (1, LANES), 1)
    ones = jnp.ones((1, LANES), F32)

    def three(value):
        first = value.astype(BF16).astype(F32)
        second = (value - first).astype(BF16).astype(F32)
        return [first, second, value - first - second]

    row_lines = [three(pot[pl.ds(here_row * rows_b + row, 1), :]) for row in range(rows_b)]
    col_lines = [three(pot[pl.ds(here_col * cols_b + col, 1), :]) for col in range(cols_b)]
    del lane
    pad = jnp.zeros((2, LANES), F32)
    left = [jnp.concatenate(value + [ones, ones, ones, pad], axis=0).astype(BF16) for value in row_lines]
    right = [jnp.concatenate([ones, ones, ones] + value + [pad], axis=0).astype(BF16) for value in col_lines]
    for step in range(ways):
        for row in range(rows_b):
            for col in range(cols_b):
                line = pattern_at + row * cols_b + col
                keep = firsts[step][line : line + 1, :].astype(BF16)
                spot = (slice(row * BLOCK, (row + 1) * BLOCK), at(col))
                block = dens[step][spot] * keep
                masked[spot] = block
                if step == 0:
                    sums = contract(left[row], right[col], ((0,), (0,)))
                    total[spot] = COUPLE * sums * block.astype(F32)
        start = pl.multiple_of((here_col ^ step) * cols, BLOCK)
        total[...] += contract(masked[...], panel[pl.ds(start, cols), :], ((1,), (0,)))
    out[...] = total[...].astype(BF16)


VMEM = pl.BlockSpec(memory_space=pltpu.VMEM)
SMEM = pl.BlockSpec(memory_space=pltpu.SMEM)


def call(kernel, name, outs, operands, scalars=0, scratch=(), cost=(0, 0)):
    return pl.pallas_call(
        kernel,
        out_shape=[jax.ShapeDtypeStruct(shape, dtype) for shape, dtype in outs],
        in_specs=[SMEM] * scalars + [VMEM] * (len(operands) - scalars),
        out_specs=[VMEM] * len(outs),
        scratch_shapes=list(scratch),
        compiler_params=pltpu.CompilerParams(vmem_limit_bytes=48 << 20),
        cost_estimate=pl.CostEstimate(flops=cost[0], bytes_accessed=cost[1], transcendentals=0),
        name=name,
    )(*operands)


def shards(
    density,
    margin,
    pattern_d,
    pattern_s,
    dipole,
    owner,
    centres,
    angles,
    velocity,
    angmom,
    halo_list,
    neighbours,
):
    rows, cols = density.shape
    rows_b, cols_b = pattern_d.shape
    rows_n = lax.axis_size("row")
    sub_n = lax.axis_size("sub")
    across = ("col", "sub")
    ways = lax.axis_size("col") * sub_n
    hist_rows = rows * rows_n // LANES
    waters, listed = centres.shape[1], halo_list.shape[1]
    where = jnp.stack([lax.axis_index("row"), lax.axis_index(across)]).astype(jnp.int32)

    def swap(value, axis, count, step):
        return lax.ppermute(value, axis, [(i, i ^ step) for i in range(count)])

    def ring(value, by):
        return lax.ppermute(value, "row", [(i, (i + by) % rows_n) for i in range(rows_n)])

    dens_all = [density]
    for step in range(1, ways):
        if step % 2 == 1 and step > 1:
            dens_all.append(swap(dens_all[step - 1], "sub", sub_n, 1))
        else:
            dens_all.append(swap(density, across, ways, step))

    depth = 8 * max(rows_b, cols_b)
    small, first, expanded = call(
        open_kernel,
        "margin_blocks_and_counts",
        [
            ((rows, BLOCK), BF16),
            ((hist_rows + depth + rows_b * cols_b, LANES), F32),
            ((rows_b * cols_b, LANES), F32),
        ],
        [pattern_d, pattern_s, margin, dipole, owner],
        scalars=2,
        cost=(10**8, 10**6),
    )
    firsts = [first] + [swap(first, across, ways, step) for step in range(1, ways)]
    small_all = [small] + [swap(small, "row", rows_n, step) for step in range(1, rows_n)]

    sites, quat, up, down = call(
        sites_kernel,
        "sites",
        [((16, waters), F32), ((4, waters), F32), ((16, listed), F32), ((16, listed), F32)],
        [centres, angles, halo_list],
        cost=(10**7, 10**6),
    )
    below, above = ring(up, 1), ring(down, -1)

    (second,) = call(
        functools.partial(gathered_kernel, ways, hist_rows),
        "row_counts",
        [((hist_rows + rows_b * cols_b, LANES), F32)],
        firsts + [expanded],
    )
    seconds = [second] + [swap(second, "row", rows_n, step) for step in range(1, rows_n)]
    pot, part = call(
        functools.partial(project_kernel, ways, rows_n, hist_rows),
        "field_parts",
        [((hist_rows, LANES), F32), ((8, cols), F32)],
        [where, pattern_d, density] + firsts + seconds,
        scalars=2,
        scratch=[pltpu.VMEM((ways, depth, LANES), F32), pltpu.VMEM((8, rows), F32), pltpu.VMEM((rows, cols), BF16)],
        cost=(10**7, 10**6),
    )
    parts = [part] + [swap(part, "row", rows_n, step) for step in range(1, rows_n)]
    (field,) = call(
        functools.partial(field_kernel, rows_n), "field", [((8, cols), F32)], [where, pot] + parts, scalars=1
    )
    fields = [field] + [swap(field, across, ways, step) for step in range(1, ways)]

    tiles = (waters + 2 * listed) // LANES
    (pair,) = call(
        pair_kernel,
        "pair_forces",
        [((9, waters), F32)],
        [sites, below, above, neighbours],
        scratch=[pltpu.VMEM((9, tiles, 8, LANES), F32)],
        cost=(10**9, 10**7),
    )
    (qm_out,) = call(
        functools.partial(product_kernel, ways, rows_n, hist_rows),
        "product",
        [((rows, cols), BF16)],
        [where, pot] + firsts + seconds + dens_all + small_all,
        scalars=1,
        scratch=[
            pltpu.VMEM((rows * rows_n, cols), BF16),
            pltpu.VMEM((rows, cols), BF16),
            pltpu.VMEM((rows, cols), F32),
        ],
        cost=(10**9, 10**7),
    )
    centres_new, velocity_new, angmom_new, orient_new = call(
        functools.partial(advance_kernel, ways),
        "advance",
        [((3, waters), F32), ((3, waters), F32), ((3, waters), F32), ((4, waters), F32)],
        [where, owner, sites, quat, pair, centres, velocity, angmom] + fields,
        scalars=1,
        scratch=[pltpu.VMEM((16, waters), F32)],
        cost=(10**7, 10**6),
    )
    return (qm_out, centres_new, velocity_new, angmom_new, orient_new)


def solution(mesh):
    square = P(("groups", "row"), ("col", "sub"))
    spread = P(None, ("groups", "row", "col", "sub"))
    return jax.shard_map(
        shards,
        mesh=mesh,
        in_specs=(square,) * 4 + (P(None, ("groups", "col", "sub")),) + (spread,) * 7,
        out_specs=(square,) + (spread,) * 4,
        check_vma=False,
    )
```

time: 418 us -> 66.7 us (0.16)
  other arithmetic: 160 us -> 0.07 us
  local copies, waits for them, and re-layouts: 130 us -> 3.84 us
  blocking collectives: 103 us -> 0 us
  waiting for transfers between devices: 0.06 us -> 25.6 us
  starting transfers between devices: 5.18 us -> 22 us
  Pallas kernels: 0 us -> 14.1 us
  between operations: 14.5 us -> 0.75 us
    reduce_sum x6 -> x0, other arithmetic: 130 us -> none  [the longest x3 94.2 us: pair_forces(): total = total + jnp.sum(offset_vec * weight[None], axis=1)]
    gather x11 -> x0, local copies, waits for them, and re-layouts: 119 us -> none  [the longest x1 108 us: shards(): partner = table[:, neighbours]]
    psum x2 -> x0, blocking collectives: 103 us -> none  [the longest x1 69.2 us: shards(): qm_field = lax.psum(spread_out, ('row', 'col', 'sub'))]
    ppermute x2 -> x20, waiting for transfers between devices: 0.01 us -> 25.6 us  [the longest x18 24.6 us: swap(): return lax.ppermute(value, axis, [(i, i ^ step) for i in range(count)])]
    ppermute x2 -> x20, starting transfers between devices: 5.1 us -> 22 us  [the longest x18 18.1 us: swap(): return lax.ppermute(value, axis, [(i, i ^ step) for i in range(count)])]
    scatter-add x1 -> x0, other arithmetic: 16.7 us -> none  [shards(): jax.ops.segment_sum(site_charge.reshape(-1), owner.reshape(-1), num_segme...]
    pallas_call x0 -> x8, Pallas kernels: none -> 14.1 us  [call(): pl.pallas_call(kernel, out_shape=[jax.ShapeDtypeStruct(shape, dtype) for...]
    reduce_sum x9 -> x0, local copies, waits for them, and re-layouts: 5.95 us -> none  [pair_forces(): total = total + jnp.sum(offset_vec * weight[None], axis=1)]
  transfers between devices with their start and end apart: 4 -> 20, of which waited for: 0 -> 8; matrix products, arithmetic and copies ran while one was open for 66% -> 0% of each run, Pallas kernels for 0% -> 16%
where the time goes in v1:
time: 66.7 us; the launch traced here: 66.3 us
  waiting for transfers between devices  25.6 us (38%)
  starting transfers between devices  22 us (33%)
  Pallas kernels  14.1 us (21%)
  local copies, waits for them, and re-layouts  3.84 us (6%)
  between operations  0.75 us (1%)
    ppermute x18, waiting for transfers between devices, swap(): return lax.ppermute(value, axis, [(i, i ^ step) for i in range(count)])  24.6 us
    ppermute x18, starting transfers between devices, swap(): return lax.ppermute(value, axis, [(i, i ^ step) for i in range(count)])  18.1 us
    pallas_call x8, Pallas kernels, call(): pl.pallas_call(kernel, out_shape=[jax.ShapeDtypeStruct(shape, dtype) for...  14.1 us
    ppermute x2, starting transfers between devices, ring(): lax.ppermute(value, 'row', [(i, (i + by) % rows_n) for i in range(rows_n)])  3.86 us
    unnamed x28, local copies, waits for them, and re-layouts  3.84 us
  transfers between devices with their start and end apart: 20, of which 8 were waited for; matrix products, arithmetic and copies ran while one was open for 0% of the time, Pallas kernels for 16%

profile of v1, /device:TPU:0, one launch (start us, length us, event | category | flops | bytes accessed | tf_op | source)
XLA Modules:
  0.0 66.3 jit_solution(12249723567111590665)
XLA Ops:
  0.6 0.0 copy-start
  0.6 3.0 %collective-permute-start.7 = (bf16[512,512]{1,0:T(8,128)(2,1)}, bf16[512,512]{1,0:T(8,128)(2,1)S(1)}, u32[]{:S(2)}, u32[]{:S(2)}) collective-permute-start(bf16[512,512]{1,0:T(8,128)(2,1)} %refs_8_.1), channel_id=1, source_target_pairs={{0,2},{1,3},{2,0},{3,1},{4,6},{5,7},{6,4},{7,5},{8,10},{9,11},{10,... | collective-permute-start | bytes 1572872 | tf_op jit(solution)/shard_map/ppermute | solution.py:377
  3.6 0.0 collective-permute-start.6
  3.6 12.1 %collective-permute-done.7.refs_10_ = bf16[512,512]{1,0:T(8,128)(2,1)S(1)} collective-permute-done((bf16[512,512]{1,0:T(8,128)(2,1)}, bf16[512,512]{1,0:T(8,128)(2,1)S(1)}, u32[]{:S(2)}, u32[]{:S(2)}) %collective-permute-start.7) | collective-permute-done | bytes 524320 | tf_op jit(solution)/shard_map/ppermute | solution.py:377
  15.8 0.0 collective-permute-start.8
  15.8 0.0 copy-start.1
  15.8 1.0 %copy-done.1 = bf16[512,512]{1,0:T(8,128)(2,1)S(1)} copy-done((bf16[512,512]{1,0:T(8,128)(2,1)S(1)}, bf16[512,512]{1,0:T(8,128)(2,1)}, u32[]{:S(2)}) %copy-start.1) | copy-done | bytes 524312
  16.8 0.7 %copy-done.2 = s32[3,1024]{1,0:T(4,128)S(1)} copy-done((s32[3,1024]{1,0:T(4,128)S(1)}, s32[3,1024]{1,0:T(4,128)}, u32[]{:S(2)}) %copy-start.2) | copy-done | bytes 12312
  17.5 0.7 %copy-done.7 = s32[4,4]{1,0:T(4,128)S(1)} copy-done((s32[4,4]{1,0:T(4,128)S(1)}, s32[4,4]{1,0:T(4,128)}, u32[]{:S(2)}) %copy-start.7) | copy-done | bytes 88
  18.2 0.7 %copy-done.9 = bf16[3,512]{1,0:T(4,128)(2,1)S(1)} copy-done((bf16[3,512]{1,0:T(4,128)(2,1)S(1)}, bf16[3,512]{1,0:T(4,128)(2,1)}, u32[]{:S(2)}) %copy-start.9) | copy-done | bytes 3096
  18.9 0.7 %copy-done.10 = s32[4,4]{1,0:T(4,128)S(1)} copy-done((s32[4,4]{1,0:T(4,128)S(1)}, s32[4,4]{1,0:T(4,128)}, u32[]{:S(2)}) %copy-start.10) | copy-done | bytes 88
  19.6 1.0 %margin_blocks_and_counts.1 = (bf16[512,128]{1,0:T(8,128)(2,1)S(1)}, f32[64,128]{1,0:T(8,128)S(1)}, f32[16,128]{1,0:T(8,128)S(1)}) custom-call(s32[4,4]{1,0:T(4,128)S(1)} %copy-done.7, s32[4,4]{1,0:T(4,128)S(1)} %copy-done.10, bf16[512,512]{1,0:T(8,128)(2,1)S(1)} %copy-done.1, bf16[3,512]{1,0:T(4,128)(2,1)S(1)} %copy-done.9, s32[3,1024]{1,0:T(4,128)S(1)} %copy-done.2), custom_call_target="tpu_custom_call" | custom-call | flops 100000000 | bytes 1000000 | tf_op jit(solution)/shard_map/margin_blocks_and_counts/pallas_call | solution.py:340
  20.6 0.5 collective-permute-start
  21.1 1.7 %collective-permute-start.1 = (f32[64,128]{1,0:T(8,128)S(1)}, f32[64,128]{1,0:T(8,128)S(1)}, u32[]{:S(2)}, u32[]{:S(2)}) collective-permute-start(f32[64,128]{1,0:T(8,128)S(1)} %get-tuple-element.18.refs_0_), channel_id=1, source_target_pairs={{0,2},{1,3},{2,0},{3,1},{4,6},{5,7},{6,4},{7,5},{8,10},{9,11},{10,... | collective-permute-start | bytes 98312 | tf_op jit(solution)/shard_map/ppermute | solution.py:377
  22.8 0.0 collective-permute-start.2
  22.8 0.0 collective-permute-done.refs_1_
  22.8 2.2 %collective-permute-done.1.refs_2_ = f32[64,128]{1,0:T(8,128)S(1)} collective-permute-done((f32[64,128]{1,0:T(8,128)S(1)}, f32[64,128]{1,0:T(8,128)S(1)}, u32[]{:S(2)}, u32[]{:S(2)}) %collective-permute-start.1) | collective-permute-done | bytes 32800 | tf_op jit(solution)/shard_map/ppermute | solution.py:377
  25.0 1.5 %collective-permute-done.2.refs_3_ = f32[64,128]{1,0:T(8,128)S(1)} collective-permute-done((f32[64,128]{1,0:T(8,128)S(1)}, f32[64,128]{1,0:T(8,128)S(1)}, u32[]{:S(2)}, u32[]{:S(2)}) %collective-permute-start.2) | collective-permute-done | bytes 32800 | tf_op jit(solution)/shard_map/ppermute | solution.py:377
  26.5 1.6 %collective-permute-start.3 = (f32[32,128]{1,0:T(8,128)S(1)}, f32[32,128]{1,0:T(8,128)S(1)}, u32[]{:S(2)}, u32[]{:S(2)}) collective-permute-start(f32[32,128]{1,0:T(8,128)S(1)} %row_counts.1.refs_4_), channel_id=1, source_target_pairs={{0,4},{4,0},{8,12},{12,8},{1,5},{5,1},{9,13},{13,9},{2,6},{6,2},{1... | collective-permute-start | bytes 49160 | tf_op jit(solution)/shard_map/ppermute | solution.py:377
  28.1 2.6 %collective-permute-start.4 = (f32[32,128]{1,0:T(8,128)S(1)}, f32[32,128]{1,0:T(8,128)S(1)}, u32[]{:S(2)}, u32[]{:S(2)}) collective-permute-start(f32[32,128]{1,0:T(8,128)S(1)} %row_counts.1.refs_4_), channel_id=1, source_target_pairs={{0,8},{4,12},{8,0},{12,4},{1,9},{5,13},{9,1},{13,5},{2,10},{6,14},... | collective-permute-start | bytes 49160 | tf_op jit(solution)/shard_map/ppermute | solution.py:377
  30.6 0.2 collective-permute-start.5
  30.9 0.1 pad_add_fusion.where
  31.0 0.0 collective-permute-done.3.refs_5_
  31.0 1.9 %collective-permute-done.4.refs_6_ = f32[32,128]{1,0:T(8,128)S(1)} collective-permute-done((f32[32,128]{1,0:T(8,128)S(1)}, f32[32,128]{1,0:T(8,128)S(1)}, u32[]{:S(2)}, u32[]{:S(2)}) %collective-permute-start.4) | collective-permute-done | bytes 16416 | tf_op jit(solution)/shard_map/ppermute | solution.py:377
  32.9 3.3 %collective-permute-done.5.refs_7_ = f32[32,128]{1,0:T(8,128)S(1)} collective-permute-done((f32[32,128]{1,0:T(8,128)S(1)}, f32[32,128]{1,0:T(8,128)S(1)}, u32[]{:S(2)}, u32[]{:S(2)}) %collective-permute-start.5) | collective-permute-done | bytes 16416 | tf_op jit(solution)/shard_map/ppermute | solution.py:377
  36.2 0.0 copy-done
  36.2 0.0 copy-done.8
  36.2 0.9 %field_parts.1 = (f32[16,128]{1,0:T(8,128)S(1)}, f32[8,512]{1,0:T(8,128)S(1)}) custom-call(s32[2]{0:T(128)S(1)} %pad_add_fusion.where, s32[4,4]{1,0:T(4,128)S(1)} %copy-done.8, bf16[512,512]{1,0:T(8,128)(2,1)S(1)} %copy-done, f32[64,128]{1,0:T(8,128)S(1)} %get-tuple-element.18.refs_0_, f32[64,128]{1,0:T(8,128)S(1)} %collective-permute-done.refs_1_, ...), custom_call_target="tpu_custom_call" | custom-call | flops 10000000 | bytes 1000000 | tf_op jit(solution)/shard_map/field_parts/pallas_call | solution.py:340
  37.1 0.0 collective-permute-start.14
  37.1 0.8 %collective-permute-start.15 = (f32[8,512]{1,0:T(8,128)S(1)}, f32[8,512]{1,0:T(8,128)S(1)}, u32[]{:S(2)}, u32[]{:S(2)}) collective-permute-start(f32[8,512]{1,0:T(8,128)S(1)} %get-tuple-element.26.refs_0_), channel_id=1, source_target_pairs={{0,8},{4,12},{8,0},{12,4},{1,9},{5,13},{9,1},{13,5},{2,10},{6,14},... | collective-permute-start | bytes 49160 | tf_op jit(solution)/shard_map/ppermute | solution.py:377
  37.9 3.6 %collective-permute-start.16 = (f32[8,512]{1,0:T(8,128)S(1)}, f32[8,512]{1,0:T(8,128)S(1)}, u32[]{:S(2)}, u32[]{:S(2)}) collective-permute-start(f32[8,512]{1,0:T(8,128)S(1)} %get-tuple-element.26.refs_0_), channel_id=1, source_target_pairs={{0,12},{4,8},{8,4},{12,0},{1,13},{5,9},{9,5},{13,1},{2,14},{6,10},... | collective-permute-start | bytes 49160 | tf_op jit(solution)/shard_map/ppermute | solution.py:377
  41.5 0.0 copy-done.4
  41.5 0.0 copy-done.12
  41.5 0.0 copy-done.13
  41.5 0.2 sites.1
  41.8 0.0 collective-permute-done.14.refs_1_
  41.8 0.1 collective-permute-start.12
  41.8 0.0 collective-permute-done.15.refs_2_
  41.8 3.8 %collective-permute-start.13 = (f32[16,256]{1,0:T(8,128)S(1)}, f32[16,256]{1,0:T(8,128)S(1)}, u32[]{:S(2)}, u32[]{:S(2)}) collective-permute-start(f32[16,256]{1,0:T(8,128)S(1)} %get-tuple-element.25), channel_id=1, source_target_pairs={{0,12},{4,0},{8,4},{12,8},{1,13},{5,1},{9,5},{13,9},{2,14},{6,2},{... | collective-permute-start | bytes 49160 | tf_op jit(solution)/shard_map/ppermute | solution.py:380
  45.7 0.0 collective-permute-done.16.refs_3_
  45.7 0.6 field.1.refs_0_
  46.2 0.1 collective-permute-start.17
  46.3 1.1 %collective-permute-done.12.below = f32[16,256]{1,0:T(8,128)S(1)} collective-permute-done((f32[16,256]{1,0:T(8,128)S(1)}, f32[16,256]{1,0:T(8,128)S(1)}, u32[]{:S(2)}, u32[]{:S(2)}) %collective-permute-start.12) | collective-permute-done | bytes 16416 | tf_op jit(solution)/shard_map/ppermute | solution.py:380
  47.4 0.7 collective-permute-start.18
  48.0 0.0 collective-permute-done.13.above
  48.0 0.1 collective-permute-start.19
  48.1 0.0 collective-permute-done.17.refs_1_
  48.2 0.0 collective-permute-start.9
  48.2 3.0 %collective-permute-done.18.refs_2_ = f32[8,512]{1,0:T(8,128)S(1)} collective-permute-done((f32[8,512]{1,0:T(8,128)S(1)}, f32[8,512]{1,0:T(8,128)S(1)}, u32[]{:S(2)}, u32[]{:S(2)}) %collective-permute-start.18) | collective-permute-done | bytes 16416 | tf_op jit(solution)/shard_map/ppermute | solution.py:377
  51.2 0.6 collective-permute-start.10
  51.8 0.0 collective-permute-done.19.refs_3_
  51.8 2.6 %collective-permute-start.11 = (bf16[512,128]{1,0:T(8,128)(2,1)S(1)}, bf16[512,128]{1,0:T(8,128)(2,1)S(1)}, u32[]{:S(2)}, u32[]{:S(2)}) collective-permute-start(bf16[512,128]{1,0:T(8,128)(2,1)S(1)} %get-tuple-element.21.refs_12_), channel_id=1, source_target_pairs={{0,12},{4,8},{8,4},{12,0},{1,13},{5,9},{9,5},{13,1},{2,14},{6,10},... | collective-permute-start | bytes 393224 | tf_op jit(solution)/shard_map/ppermute | solution.py:377
  54.4 0.0 copy-done.11
  54.4 6.3 %pair_forces.1.pair = f32[9,1024]{1,0:T(8,128)S(1)} custom-call(f32[16,1024]{1,0:T(8,128)S(1)} %get-tuple-element.22.sites, f32[16,256]{1,0:T(8,128)S(1)} %collective-permute-done.12.below, f32[16,256]{1,0:T(8,128)S(1)} %collective-permute-done.13.above, s32[32,1024]{1,0:T(8,128)S(1)} %copy-done.11), custom_call_target="tpu_custom_call" | custom-call | flops 1000000000 | bytes 10000000 | tf_op jit(solution)/shard_map/pair_forces/pallas_call | solution.py:340
  60.6 0.0 copy-done.3
  60.7 0.0 copy-done.5
  60.7 0.0 copy-done.6
  60.7 1.8 %advance.1 = (f32[3,1024]{1,0:T(4,128)}, f32[3,1024]{1,0:T(4,128)}, f32[3,1024]{1,0:T(4,128)}, f32[4,1024]{1,0:T(4,128)}) custom-call(s32[2]{0:T(128)S(1)} %pad_add_fusion.where, s32[3,1024]{1,0:T(4,128)S(1)} %copy-done.3, f32[16,1024]{1,0:T(8,128)S(1)} %get-tuple-element.22.sites, f32[4,1024]{1,0:T(4,128)S(1)} %get-tuple-element.23.quat, ...), custom_call_target="tpu_custom_call" | custom-call | flops 10000000 | bytes 1000000 | tf_op jit(solution)/shard_map/advance/pallas_call | solution.py:340
  62.5 0.0 collective-permute-done.9.refs_13_
  62.5 0.5 collective-permute-done.10.refs_14_
  63.0 0.0 collective-permute-done.11.refs_15_
  63.0 0.0 collective-permute-done.6.refs_9_
  63.0 0.0 collective-permute-done.8.refs_11_
  63.0 3.3 %product.1 = bf16[512,512]{1,0:T(8,128)(2,1)} custom-call(s32[2]{0:T(128)S(1)} %pad_add_fusion.where, f32[16,128]{1,0:T(8,128)S(1)} %get-tuple-element.20.pot, f32[64,128]{1,0:T(8,128)S(1)} %get-tuple-element.18.refs_0_, f32[64,128]{1,0:T(8,128)S(1)} %collective-permute-done.refs_1_, f32[64,128]{1,0:T(8,128)S(1)} %collective-permute-done.1.refs_2_, ...), custom_call_target="tpu_custom_call" | custom-call | flops 1000000000 | bytes 10000000 | tf_op jit(solution)/shard_map/product/pallas_call | solution.py:340
  (13 shorter events, 0.0 us)
Async XLA Ops:
  0.6 35.6 %copy-start = (bf16[512,512]{1,0:T(8,128)(2,1)S(1)}, bf16[512,512]{1,0:T(8,128)(2,1)}, u32[]{:S(2)}) copy-start(bf16[512,512]{1,0:T(8,128)(2,1)} %refs_8_.1) | copy-start | bytes 1572868
  0.6 15.1 %collective-permute-start.7 = (bf16[512,512]{1,0:T(8,128)(2,1)}, bf16[512,512]{1,0:T(8,128)(2,1)S(1)}, u32[]{:S(2)}, u32[]{:S(2)}) collective-permute-start(bf16[512,512]{1,0:T(8,128)(2,1)} %refs_8_.1), channel_id=1, source_target_pairs={{0,2},{1,3},{2,0},{3,1},{4,6},{5,7},{6,4},{7,5},{8,10},{9,11},{10,... | collective-permute-start | bytes 1572872 | tf_op jit(solution)/shard_map/ppermute | solution.py:377
  3.6 59.3 %collective-permute-start.6 = (bf16[512,512]{1,0:T(8,128)(2,1)}, bf16[512,512]{1,0:T(8,128)(2,1)S(1)}, u32[]{:S(2)}, u32[]{:S(2)}) collective-permute-start(bf16[512,512]{1,0:T(8,128)(2,1)} %refs_8_.1), channel_id=1, source_target_pairs={{0,1},{1,0},{2,3},{3,2},{4,5},{5,4},{6,7},{7,6},{8,9},{9,8},{10,11... | collective-permute-start | bytes 1572872 | tf_op jit(solution)/shard_map/ppermute | solution.py:377
  15.8 47.2 %collective-permute-start.8 = (bf16[512,512]{1,0:T(8,128)(2,1)S(1)}, bf16[512,512]{1,0:T(8,128)(2,1)S(1)}, u32[]{:S(2)}, u32[]{:S(2)}) collective-permute-start(bf16[512,512]{1,0:T(8,128)(2,1)S(1)} %collective-permute-done.7.refs_10_), channel_id=1, source_target_pairs={{0,1},{1,0},{2,3},{3,2},{4,5},{5,4},{6,7},{7,6},{8,9},{9,8},{10,11... | collective-permute-start | bytes 1572872 | tf_op jit(solution)/shard_map/ppermute | solution.py:377
  15.8 1.0 %copy-start.1 = (bf16[512,512]{1,0:T(8,128)(2,1)S(1)}, bf16[512,512]{1,0:T(8,128)(2,1)}, u32[]{:S(2)}) copy-start(bf16[512,512]{1,0:T(8,128)(2,1)} %marg.1) | copy-start | bytes 1572868
  16.8 0.7 %copy-start.2 = (s32[3,1024]{1,0:T(4,128)S(1)}, s32[3,1024]{1,0:T(4,128)}, u32[]{:S(2)}) copy-start(s32[3,1024]{1,0:T(4,128)} %owner.3) | copy-start | bytes 36868
  17.5 0.7 %copy-start.7 = (s32[4,4]{1,0:T(4,128)S(1)}, s32[4,4]{1,0:T(4,128)}, u32[]{:S(2)}) copy-start(s32[4,4]{1,0:T(4,128)} %pat_d.3) | copy-start | bytes 196
  18.2 0.7 %copy-start.9 = (bf16[3,512]{1,0:T(4,128)(2,1)S(1)}, bf16[3,512]{1,0:T(4,128)(2,1)}, u32[]{:S(2)}) copy-start(bf16[3,512]{1,0:T(4,128)(2,1)} %dip.1) | copy-start | bytes 9220
  18.9 0.7 %copy-start.10 = (s32[4,4]{1,0:T(4,128)S(1)}, s32[4,4]{1,0:T(4,128)}, u32[]{:S(2)}) copy-start(s32[4,4]{1,0:T(4,128)} %pat_s.1) | copy-start | bytes 196
  20.6 2.3 %collective-permute-start = (f32[64,128]{1,0:T(8,128)S(1)}, f32[64,128]{1,0:T(8,128)S(1)}, u32[]{:S(2)}, u32[]{:S(2)}) collective-permute-start(f32[64,128]{1,0:T(8,128)S(1)} %get-tuple-element.18.refs_0_), channel_id=1, source_target_pairs={{0,1},{1,0},{2,3},{3,2},{4,5},{5,4},{6,7},{7,6},{8,9},{9,8},{10,11... | collective-permute-start | bytes 98312 | tf_op jit(solution)/shard_map/ppermute | solution.py:377
  21.1 3.9 %collective-permute-start.1 = (f32[64,128]{1,0:T(8,128)S(1)}, f32[64,128]{1,0:T(8,128)S(1)}, u32[]{:S(2)}, u32[]{:S(2)}) collective-permute-start(f32[64,128]{1,0:T(8,128)S(1)} %get-tuple-element.18.refs_0_), channel_id=1, source_target_pairs={{0,2},{1,3},{2,0},{3,1},{4,6},{5,7},{6,4},{7,5},{8,10},{9,11},{10,... | collective-permute-start | bytes 98312 | tf_op jit(solution)/shard_map/ppermute | solution.py:377
  22.8 3.6 %collective-permute-start.2 = (f32[64,128]{1,0:T(8,128)S(1)}, f32[64,128]{1,0:T(8,128)S(1)}, u32[]{:S(2)}, u32[]{:S(2)}) collective-permute-start(f32[64,128]{1,0:T(8,128)S(1)} %get-tuple-element.18.refs_0_), channel_id=1, source_target_pairs={{0,3},{1,2},{2,1},{3,0},{4,7},{5,6},{6,5},{7,4},{8,11},{9,10},{10,... | collective-permute-start | bytes 98312 | tf_op jit(solution)/shard_map/ppermute | solution.py:377
  26.5 4.5 %collective-permute-start.3 = (f32[32,128]{1,0:T(8,128)S(1)}, f32[32,128]{1,0:T(8,128)S(1)}, u32[]{:S(2)}, u32[]{:S(2)}) collective-permute-start(f32[32,128]{1,0:T(8,128)S(1)} %row_counts.1.refs_4_), channel_id=1, source_target_pairs={{0,4},{4,0},{8,12},{12,8},{1,5},{5,1},{9,13},{13,9},{2,6},{6,2},{1... | collective-permute-start | bytes 49160 | tf_op jit(solution)/shard_map/ppermute | solution.py:377
  28.1 4.8 %collective-permute-start.4 = (f32[32,128]{1,0:T(8,128)S(1)}, f32[32,128]{1,0:T(8,128)S(1)}, u32[]{:S(2)}, u32[]{:S(2)}) collective-permute-start(f32[32,128]{1,0:T(8,128)S(1)} %row_counts.1.refs_4_), channel_id=1, source_target_pairs={{0,8},{4,12},{8,0},{12,4},{1,9},{5,13},{9,1},{13,5},{2,10},{6,14},... | collective-permute-start | bytes 49160 | tf_op jit(solution)/shard_map/ppermute | solution.py:377
  30.6 5.5 %collective-permute-start.5 = (f32[32,128]{1,0:T(8,128)S(1)}, f32[32,128]{1,0:T(8,128)S(1)}, u32[]{:S(2)}, u32[]{:S(2)}) collective-permute-start(f32[32,128]{1,0:T(8,128)S(1)} %row_counts.1.refs_4_), channel_id=1, source_target_pairs={{0,12},{4,8},{8,4},{12,0},{1,13},{5,9},{9,5},{13,1},{2,14},{6,10},... | collective-permute-start | bytes 49160 | tf_op jit(solution)/shard_map/ppermute | solution.py:377
  30.9 5.3 %copy-start.8 = (s32[4,4]{1,0:T(4,128)S(1)}, s32[4,4]{1,0:T(4,128)}, u32[]{:S(2)}) copy-start(s32[4,4]{1,0:T(4,128)} %pat_d.3) | copy-start | bytes 196
  30.9 10.6 %copy-start.4 = (f32[3,1024]{1,0:T(4,128)S(1)}, f32[3,1024]{1,0:T(4,128)}, u32[]{:S(2)}) copy-start(f32[3,1024]{1,0:T(4,128)} %centres.3) | copy-start | bytes 36868
  30.9 10.6 %copy-start.12 = (f32[3,1024]{1,0:T(4,128)S(1)}, f32[3,1024]{1,0:T(4,128)}, u32[]{:S(2)}) copy-start(f32[3,1024]{1,0:T(4,128)} %angles.1) | copy-start | bytes 36868
  30.9 10.6 %copy-start.13 = (s32[2,256]{1,0:T(2,128)S(1)}, s32[2,256]{1,0:T(2,128)}, u32[]{:S(2)}) copy-start(s32[2,256]{1,0:T(2,128)} %halo.1) | copy-start | bytes 6148
  37.1 17.2 %copy-start.11 = (s32[32,1024]{1,0:T(8,128)S(1)}, s32[32,1024]{1,0:T(8,128)}, u32[]{:S(2)}) copy-start(s32[32,1024]{1,0:T(8,128)} %neighbours.1) | copy-start | bytes 393220
  37.1 4.6 %collective-permute-start.14 = (f32[8,512]{1,0:T(8,128)S(1)}, f32[8,512]{1,0:T(8,128)S(1)}, u32[]{:S(2)}, u32[]{:S(2)}) collective-permute-start(f32[8,512]{1,0:T(8,128)S(1)} %get-tuple-element.26.refs_0_), channel_id=1, source_target_pairs={{0,4},{4,0},{8,12},{12,8},{1,5},{5,1},{9,13},{13,9},{2,6},{6,2},{1... | collective-permute-start | bytes 49160 | tf_op jit(solution)/shard_map/ppermute | solution.py:377
  37.1 4.7 %collective-permute-start.15 = (f32[8,512]{1,0:T(8,128)S(1)}, f32[8,512]{1,0:T(8,128)S(1)}, u32[]{:S(2)}, u32[]{:S(2)}) collective-permute-start(f32[8,512]{1,0:T(8,128)S(1)} %get-tuple-element.26.refs_0_), channel_id=1, source_target_pairs={{0,8},{4,12},{8,0},{12,4},{1,9},{5,13},{9,1},{13,5},{2,10},{6,14},... | collective-permute-start | bytes 49160 | tf_op jit(solution)/shard_map/ppermute | solution.py:377
  37.9 7.7 %collective-permute-start.16 = (f32[8,512]{1,0:T(8,128)S(1)}, f32[8,512]{1,0:T(8,128)S(1)}, u32[]{:S(2)}, u32[]{:S(2)}) collective-permute-start(f32[8,512]{1,0:T(8,128)S(1)} %get-tuple-element.26.refs_0_), channel_id=1, source_target_pairs={{0,12},{4,8},{8,4},{12,0},{1,13},{5,9},{9,5},{13,1},{2,14},{6,10},... | collective-permute-start | bytes 49160 | tf_op jit(solution)/shard_map/ppermute | solution.py:377
  41.8 5.6 %collective-permute-start.12 = (f32[16,256]{1,0:T(8,128)S(1)}, f32[16,256]{1,0:T(8,128)S(1)}, u32[]{:S(2)}, u32[]{:S(2)}) collective-permute-start(f32[16,256]{1,0:T(8,128)S(1)} %get-tuple-element.24), channel_id=1, source_target_pairs={{0,4},{4,8},{8,12},{12,0},{1,5},{5,9},{9,13},{13,1},{2,6},{6,10},{... | collective-permute-start | bytes 49160 | tf_op jit(solution)/shard_map/ppermute | solution.py:380
  41.8 6.2 %collective-permute-start.13 = (f32[16,256]{1,0:T(8,128)S(1)}, f32[16,256]{1,0:T(8,128)S(1)}, u32[]{:S(2)}, u32[]{:S(2)}) collective-permute-start(f32[16,256]{1,0:T(8,128)S(1)} %get-tuple-element.25), channel_id=1, source_target_pairs={{0,12},{4,0},{8,4},{12,8},{1,13},{5,1},{9,5},{13,9},{2,14},{6,2},{... | collective-permute-start | bytes 49160 | tf_op jit(solution)/shard_map/ppermute | solution.py:380
  46.2 1.9 %collective-permute-start.17 = (f32[8,512]{1,0:T(8,128)S(1)}, f32[8,512]{1,0:T(8,128)S(1)}, u32[]{:S(2)}, u32[]{:S(2)}) collective-permute-start(f32[8,512]{1,0:T(8,128)S(1)} %field.1.refs_0_), channel_id=1, source_target_pairs={{0,1},{1,0},{2,3},{3,2},{4,5},{5,4},{6,7},{7,6},{8,9},{9,8},{10,11... | collective-permute-start | bytes 49160 | tf_op jit(solution)/shard_map/ppermute | solution.py:377
  47.4 3.8 %collective-permute-start.18 = (f32[8,512]{1,0:T(8,128)S(1)}, f32[8,512]{1,0:T(8,128)S(1)}, u32[]{:S(2)}, u32[]{:S(2)}) collective-permute-start(f32[8,512]{1,0:T(8,128)S(1)} %field.1.refs_0_), channel_id=1, source_target_pairs={{0,2},{1,3},{2,0},{3,1},{4,6},{5,7},{6,4},{7,5},{8,10},{9,11},{10,... | collective-permute-start | bytes 49160 | tf_op jit(solution)/shard_map/ppermute | solution.py:377
  48.0 3.7 %collective-permute-start.19 = (f32[8,512]{1,0:T(8,128)S(1)}, f32[8,512]{1,0:T(8,128)S(1)}, u32[]{:S(2)}, u32[]{:S(2)}) collective-permute-start(f32[8,512]{1,0:T(8,128)S(1)} %field.1.refs_0_), channel_id=1, source_target_pairs={{0,3},{1,2},{2,1},{3,0},{4,7},{5,6},{6,5},{7,4},{8,11},{9,10},{10,... | collective-permute-start | bytes 49160 | tf_op jit(solution)/shard_map/ppermute | solution.py:377
  48.2 14.3 %collective-permute-start.9 = (bf16[512,128]{1,0:T(8,128)(2,1)S(1)}, bf16[512,128]{1,0:T(8,128)(2,1)S(1)}, u32[]{:S(2)}, u32[]{:S(2)}) collective-permute-start(bf16[512,128]{1,0:T(8,128)(2,1)S(1)} %get-tuple-element.21.refs_12_), channel_id=1, source_target_pairs={{0,4},{4,0},{8,12},{12,8},{1,5},{5,1},{9,13},{13,9},{2,6},{6,2},{1... | collective-permute-start | bytes 393224 | tf_op jit(solution)/shard_map/ppermute | solution.py:377
  51.2 11.8 %collective-permute-start.10 = (bf16[512,128]{1,0:T(8,128)(2,1)S(1)}, bf16[512,128]{1,0:T(8,128)(2,1)S(1)}, u32[]{:S(2)}, u32[]{:S(2)}) collective-permute-start(bf16[512,128]{1,0:T(8,128)(2,1)S(1)} %get-tuple-element.21.refs_12_), channel_id=1, source_target_pairs={{0,8},{4,12},{8,0},{12,4},{1,9},{5,13},{9,1},{13,5},{2,10},{6,14},... | collective-permute-start | bytes 393224 | tf_op jit(solution)/shard_map/ppermute | solution.py:377
  51.8 11.2 %collective-permute-start.11 = (bf16[512,128]{1,0:T(8,128)(2,1)S(1)}, bf16[512,128]{1,0:T(8,128)(2,1)S(1)}, u32[]{:S(2)}, u32[]{:S(2)}) collective-permute-start(bf16[512,128]{1,0:T(8,128)(2,1)S(1)} %get-tuple-element.21.refs_12_), channel_id=1, source_target_pairs={{0,12},{4,8},{8,4},{12,0},{1,13},{5,9},{9,5},{13,1},{2,14},{6,10},... | collective-permute-start | bytes 393224 | tf_op jit(solution)/shard_map/ppermute | solution.py:377
  54.4 6.3 %copy-start.3 = (s32[3,1024]{1,0:T(4,128)S(1)}, s32[3,1024]{1,0:T(4,128)}, u32[]{:S(2)}) copy-start(s32[3,1024]{1,0:T(4,128)} %owner.3) | copy-start | bytes 36868
  54.4 6.3 %copy-start.5 = (f32[3,1024]{1,0:T(4,128)S(1)}, f32[3,1024]{1,0:T(4,128)}, u32[]{:S(2)}) copy-start(f32[3,1024]{1,0:T(4,128)} %velocity.1) | copy-start | bytes 36868
  54.4 6.3 %copy-start.6 = (f32[3,1024]{1,0:T(4,128)S(1)}, f32[3,1024]{1,0:T(4,128)}, u32[]{:S(2)}) copy-start(f32[3,1024]{1,0:T(4,128)} %angmom.1) | copy-start | bytes 36868

commit v2 on v1

v2 whole, which is shorter than its diff:
```python
import functools

import jax
import jax.numpy as jnp
from jax import lax
from jax.experimental import pallas as pl
from jax.experimental.pallas import tpu as pltpu
from jax.sharding import PartitionSpec as P

BLOCK = 128
LANES = 128

CHARGE = (-0.834, 0.417, 0.417)
UNIT = 0.417
MULTIPLE = (-2.0, 1.0, 1.0)
OFFSET = ((0.0, 0.0, -0.12), (0.76, 0.0, 0.47), (-0.76, 0.0, 0.47))
COUPLE = 0.1
STEP_DT = 0.5
WATER_MASS = 1.0
INERTIA = 0.5
SOFTEN = 1.0

F32 = jnp.float32
BF16 = jnp.bfloat16

SIN_TERMS = (-1 / 6, 1 / 120, -1 / 5040, 1 / 362880, -1 / 39916800, 1 / 6227020800)
COS_TERMS = (-1 / 2, 1 / 24, -1 / 720, 1 / 40320, -1 / 3628800, 1 / 479001600, -1 / 87178291200)


def at(tile):
    return slice(tile * LANES, (tile + 1) * LANES)


def pick(table, index):
    return jnp.take_along_axis(table, index, axis=1, mode="promise_in_bounds")


def contract(left, right, dims):
    return lax.dot_general(left, right, (dims, ((), ())), preferred_element_type=F32)


def series(square, terms):
    total = jnp.full_like(square, terms[-1])
    for term in terms[-2::-1]:
        total = total * square + term
    return total * square + 1.0


def slot_rows(rows_b, cols_b):
    pattern_at = rows_b + cols_b
    product_at = pattern_at + 1
    return pattern_at, product_at, -(-(product_at + 3 * rows_b) // 8) * 8


def open_kernel(
    ways, rows_n, where, pat_d, pat_s, marg, dip, owner, centres, angles, halo, message, small, sites, quat, shared, count
):
    rows_b, cols_b = pat_d.shape
    pattern_at, product_at, depth = slot_rows(rows_b, cols_b)
    rows = marg.shape[0]
    lane = lax.broadcasted_iota(jnp.int32, (1, LANES), 1)
    patterns = jnp.zeros((1, LANES), F32)
    products = []
    for row in range(rows_b):
        chosen = jnp.int32(0)
        for col in range(cols_b):
            chosen = chosen + col * pat_s[row, col]
            line = row * cols_b + col
            patterns = jnp.where(lane == line, pat_d[row, col].astype(F32), patterns)
            patterns = jnp.where(lane == rows_b * cols_b + line, pat_s[row, col].astype(F32), patterns)
        span = pl.ds(pl.multiple_of(chosen * BLOCK, BLOCK), BLOCK)
        block = marg[row * BLOCK : (row + 1) * BLOCK, span]
        for copy in range(rows_n):
            small[copy * rows + row * BLOCK : copy * rows + (row + 1) * BLOCK, :] = block
        products.append(contract(dip[:, span], block, ((1,), (1,))))
    waters = owner.shape[1]
    hist_rows = count.shape[0]
    total = jnp.zeros(count.shape, F32)
    for source in range(3):
        line = owner[source : source + 1, :]
        high = lax.broadcasted_iota(jnp.int32, (hist_rows, waters), 0) == (line >> 7)
        low = lax.broadcasted_iota(jnp.int32, (LANES, waters), 0) == (line & 127)
        total = total + contract(
            jnp.where(high, MULTIPLE[source], 0.0).astype(BF16),
            jnp.where(low, 1.0, 0.0).astype(BF16),
            ((1,), (1,)),
        )
    count[...] = total
    message[...] = jnp.zeros(message.shape, F32)
    for device in range(rows_n * ways):
        base = device * depth
        row, col = device // ways, device % ways
        message[base : base + rows_b, :] = count[row * rows_b : (row + 1) * rows_b, :]
        message[base + rows_b : base + pattern_at, :] = count[col * cols_b : (col + 1) * cols_b, :]
        message[base + pattern_at : base + product_at, :] = patterns
        for block in range(rows_b):
            start = base + product_at + 3 * block
            message[start : start + 3, :] = products[block]
    water_sites(rows_n, where[0], centres, angles, halo, sites, quat, shared)


def project_kernel(ways, rows_n, where, pat_d, dens, dip, received, out, pot, lines, masked):
    rows_b, cols_b = pat_d.shape
    pattern_at, product_at, depth = slot_rows(rows_b, cols_b)
    here_col = where[1]
    total = jnp.zeros((pattern_at, LANES), F32)
    for device in range(rows_n * ways):
        total = total + received[device * depth : device * depth + pattern_at, :]
    pot[0:pattern_at, :] = UNIT * total
    lines[...] = jnp.zeros(lines.shape, F32)
    for part in range(cols_b // rows_b):
        summed = jnp.zeros((depth, LANES), F32)
        for other in range(ways):
            source = ((here_col * (cols_b // rows_b) + part) * ways + other) * depth
            summed = summed + received[pl.ds(pl.multiple_of(source, 8), depth), :]
        for block in range(rows_b):
            col = part * rows_b + block
            moment = dip[:, at(col)].astype(F32)
            start = product_at + 3 * block
            lines[0:3, at(col)] = summed[start : start + 3] + COUPLE * pot[rows_b + col : rows_b + col + 1, :] * moment
            lines[3:6, at(col)] = moment
    for row in range(rows_b):
        for col in range(cols_b):
            block = dens[row * BLOCK : (row + 1) * BLOCK, at(col)]
            masked[row * BLOCK : (row + 1) * BLOCK, at(col)] = jnp.where(
                pat_d[row, col] != 0, block, jnp.zeros_like(block)
            )
    whole = lines[...]
    first = whole.astype(BF16)
    second = (whole - first.astype(F32)).astype(BF16)
    result = contract(first, masked[...], ((1,), (1,))) + contract(second, masked[...], ((1,), (1,)))
    out_depth = out.shape[0] // (rows_n * ways)
    for row in range(rows_b):
        field = result[0:3, at(row)] + COUPLE * pot[row : row + 1, :] * result[3:6, at(row)]
        for device in range(rows_n * ways):
            start = device * out_depth + 3 * row
            out[start : start + 3, :] = field


def water_sites(rows_n, here_row, centres, angles, halo, sites, quat, shared):
    half_angle = 0.5 * angles[...]
    square = half_angle * half_angle
    sine = half_angle * series(square, SIN_TERMS)
    cosine = series(square, COS_TERMS)
    sin_r, sin_p, sin_y = sine[0:1], sine[1:2], sine[2:3]
    cos_r, cos_p, cos_y = cosine[0:1], cosine[1:2], cosine[2:3]
    comp_w = cos_r * cos_p * cos_y + sin_r * sin_p * sin_y
    comp_x = sin_r * cos_p * cos_y - cos_r * sin_p * sin_y
    comp_y = cos_r * sin_p * cos_y + sin_r * cos_p * sin_y
    comp_z = cos_r * cos_p * sin_y - sin_r * sin_p * cos_y
    for place, comp in enumerate((comp_w, comp_x, comp_y, comp_z)):
        quat[place : place + 1, :] = comp
    first = (
        1.0 - 2.0 * (comp_y * comp_y + comp_z * comp_z),
        2.0 * (comp_x * comp_y + comp_w * comp_z),
        2.0 * (comp_x * comp_z - comp_w * comp_y),
    )
    third = (
        2.0 * (comp_x * comp_z + comp_w * comp_y),
        2.0 * (comp_y * comp_z - comp_w * comp_x),
        1.0 - 2.0 * (comp_x * comp_x + comp_y * comp_y),
    )
    sites[...] = jnp.zeros(sites.shape, F32)
    for source in range(3):
        for compo in range(3):
            place = 3 * source + compo
            position = centres[compo : compo + 1, :] + third[compo] * OFFSET[source][2]
            if OFFSET[source][0] != 0.0:
                position = position + first[compo] * OFFSET[source][0]
            sites[place : place + 1, :] = position
    waters, listed = centres.shape[1], halo.shape[1]
    shared[...] = jnp.zeros(shared.shape, F32)
    for which in range(2):
        other = lax.rem(here_row + (1, rows_n - 1)[which], rows_n)
        for tile in range(listed // LANES):
            index = jnp.broadcast_to(halo[which : which + 1, at(tile)], (8, LANES))
            low, high = index & 127, index >> 7
            for part in range(2):
                found = jnp.zeros((8, LANES), F32)
                for source in range(waters // LANES):
                    value = pick(sites[8 * part : 8 * part + 8, at(source)], low)
                    found = jnp.where(high == source, value, found)
                shared[pl.ds(pl.multiple_of(16 * other + 8 * part, 8), 8), at(tile)] = found


def pair_kernel(rows_n, where, sites, received, neighbours, force, table):
    waters, listed, slots = sites.shape[1], received.shape[1], neighbours.shape[0]
    below = pl.multiple_of(16 * lax.rem(where[0] + rows_n - 1, rows_n), 16)
    above = pl.multiple_of(16 * lax.rem(where[0] + 1, rows_n), 16)
    own_tiles, halo_tiles = waters // LANES, listed // LANES
    tiles = own_tiles + 2 * halo_tiles
    for tile in range(tiles):
        if tile < own_tiles:
            lines = sites[:, at(tile)]
        elif tile < own_tiles + halo_tiles:
            lines = received[pl.ds(below, 16), at(tile - own_tiles)]
        else:
            lines = received[pl.ds(above, 16), at(tile - own_tiles - halo_tiles)]
        for word in range(9):
            table[word, tile] = jnp.broadcast_to(lines[word : word + 1], (8, LANES))

    def one_tile(tile, carry):
        span = pl.ds(pl.multiple_of(tile * LANES, LANES), LANES)
        near = [jnp.zeros((8, LANES), F32) for _ in range(9)]
        far = [jnp.zeros((8, LANES), F32) for _ in range(9)]
        for pair in range(slots // 16):
            index = [neighbours[16 * pair + 8 * part : 16 * pair + 8 * part + 8, span] for part in range(2)]
            low = [value & 127 for value in index]
            high = [value >> 7 for value in index]
            found = [[None, None] for _ in range(9)]
            for source in range(tiles):
                here = [value == source for value in high]
                for word in range(9):
                    line = table[word, source]
                    for part in range(2):
                        value = pick(line, low[part])
                        found[word][part] = (
                            value if source == 0 else jnp.where(here[part], value, found[word][part])
                        )
            for part in range(2):
                for source in range(3):
                    own = [table[3 * source + compo, tile] for compo in range(3)]
                    for target in range(3):
                        gap = [own[compo] - found[3 * target + compo][part] for compo in range(3)]
                        root = lax.rsqrt(gap[0] * gap[0] + gap[1] * gap[1] + gap[2] * gap[2] + SOFTEN)
                        weight = root * root * root
                        sums = near if target == 0 else far
                        for compo in range(3):
                            sums[3 * source + compo] = sums[3 * source + compo] + gap[compo] * weight
        for place in range(9):
            factor = CHARGE[place // 3] * UNIT
            total = factor * (far[place] - 2.0 * near[place])
            force[place : place + 1, span] = jnp.sum(total, axis=0, keepdims=True)
        return carry

    lax.fori_loop(0, own_tiles, one_tile, 0)


def advance_kernel(
    ways,
    rows_n,
    rows_b,
    received,
    owner,
    sites,
    quat,
    pair,
    centres,
    velocity,
    angmom,
    centres_new,
    velocity_new,
    angmom_new,
    orient_new,
    force,
    table,
):
    waters = owner.shape[1]
    depth = received.shape[0] // (rows_n * ways)
    for row in range(rows_n):
        summed = received[row * ways * depth : (row * ways + 1) * depth, :]
        for other in range(1, ways):
            start = (row * ways + other) * depth
            summed = summed + received[start : start + depth, :]
        for block in range(rows_b):
            start = 8 * (row * rows_b + block)
            table[start : start + 3, :] = summed[3 * block : 3 * block + 3]
            table[start + 3 : start + 8, :] = jnp.zeros((5, LANES), F32)
    for tile in range(waters // LANES):
        for source in range(3):
            index = jnp.broadcast_to(owner[source : source + 1, at(tile)], (8, LANES))
            low, high = index & 127, index >> 7
            found = jnp.zeros((8, LANES), F32)
            for block in range(rows_n * rows_b):
                value = pick(table[8 * block : 8 * block + 8, :], low)
                found = jnp.where(high == block, value, found)
            lines = slice(3 * source, 3 * source + 3)
            force[lines, at(tile)] = pair[lines, at(tile)] + CHARGE[source] * found[0:3]

    def cross(left, right):
        return [
            left[1] * right[2] - left[2] * right[1],
            left[2] * right[0] - left[0] * right[2],
            left[0] * right[1] - left[1] * right[0],
        ]

    def split(array):
        return [array[compo : compo + 1, :] for compo in range(3)]

    total = force[0:3, :] + force[3:6, :] + force[6:9, :]
    torque = None
    centre = split(centres)
    for source in range(3):
        lever = [sites[3 * source + compo : 3 * source + compo + 1, :] - centre[compo] for compo in range(3)]
        push = [force[3 * source + compo : 3 * source + compo + 1, :] for compo in range(3)]
        turn = cross(lever, push)
        torque = turn if torque is None else [old + new for old, new in zip(torque, turn)]
    moving = velocity[...] + STEP_DT * total / WATER_MASS
    velocity_new[...] = moving
    centres_new[...] = centres[...] + STEP_DT * moving
    spin = [angmom[compo : compo + 1, :] + STEP_DT * torque[compo] for compo in range(3)]
    for compo in range(3):
        angmom_new[compo : compo + 1, :] = spin[compo]
    omega = [value * (1.0 / INERTIA) for value in spin]
    scalar = quat[0:1, :]
    vector = [quat[compo + 1 : compo + 2, :] for compo in range(3)]
    delta = [-(omega[0] * vector[0] + omega[1] * vector[1] + omega[2] * vector[2])]
    turned = cross(omega, vector)
    delta = delta + [scalar * omega[compo] + turned[compo] for compo in range(3)]
    moved = [old + 0.5 * STEP_DT * new for old, new in zip([scalar] + vector, delta)]
    length = jnp.sqrt(moved[0] * moved[0] + moved[1] * moved[1] + moved[2] * moved[2] + moved[3] * moved[3])
    for place in range(4):
        orient_new[place : place + 1, :] = moved[place] / length


def product_kernel(ways, rows_n, where, pot, received, small, *refs):
    dens = refs[:ways]
    out, panel, masked, total = refs[ways:]
    rows, cols = out.shape
    rows_b, cols_b = rows // BLOCK, cols // BLOCK
    pattern_at, _, depth = slot_rows(rows_b, cols_b)
    here_row, here_col = where[0], where[1]

    def patterns(row, col):
        start = pl.multiple_of((row * ways + col) * depth, 8)
        line = received[pl.ds(start, depth), :][pattern_at : pattern_at + 1]
        return jnp.broadcast_to(line, (8, LANES))

    def flag(lines, place):
        wide = pick(lines, jnp.full((8, LANES), place, jnp.int32))
        return wide[0:1].astype(BF16)

    for other in range(rows_n):
        lines = patterns(other, here_col)
        for row in range(rows_b):
            span = slice(other * rows + row * BLOCK, other * rows + (row + 1) * BLOCK)
            block = small[span, :]
            for col in range(cols_b):
                panel[span, at(col)] = block * flag(lines, rows_b * cols_b + row * cols_b + col)
    ones = jnp.ones((1, LANES), F32)

    def three(value):
        first = value.astype(BF16).astype(F32)
        second = (value - first).astype(BF16).astype(F32)
        return [first, second, value - first - second]

    row_lines = [three(pot[row : row + 1, :]) for row in range(rows_b)]
    col_lines = [three(pot[rows_b + col : rows_b + col + 1, :]) for col in range(cols_b)]
    pad = jnp.zeros((2, LANES), F32)
    left = [jnp.concatenate(value + [ones, ones, ones, pad], axis=0).astype(BF16) for value in row_lines]
    right = [jnp.concatenate([ones, ones, ones] + value + [pad], axis=0).astype(BF16) for value in col_lines]
    for step in range(ways):
        lines = patterns(here_row, here_col ^ step)
        for row in range(rows_b):
            for col in range(cols_b):
                spot = (slice(row * BLOCK, (row + 1) * BLOCK), at(col))
                block = dens[step][spot] * flag(lines, row * cols_b + col)
                masked[spot] = block
                if step == 0:
                    sums = contract(left[row], right[col], ((0,), (0,)))
                    total[spot] = COUPLE * sums * block.astype(F32)
        start = pl.multiple_of((here_col ^ step) * cols, BLOCK)
        total[...] += contract(masked[...], panel[pl.ds(start, cols), :], ((1,), (0,)))
    out[...] = total[...].astype(BF16)


def tie_kernel(first, second, out):
    pass


VMEM = pl.BlockSpec(memory_space=pltpu.VMEM)
SMEM = pl.BlockSpec(memory_space=pltpu.SMEM)


def fetching(kernel, places, *refs):
    refs, semaphore = list(refs[:-1]), refs[-1]
    held = refs[len(refs) - len(places) :]
    copies = [pltpu.make_async_copy(refs[at_], held[n], semaphore.at[n]) for n, at_ in enumerate(places)]
    for copy in copies:
        copy.start()
    for copy in copies:
        copy.wait()
    for n, at_ in enumerate(places):
        refs[at_] = held[n]
    kernel(*refs[: len(refs) - len(places)])


def call(
    kernel, name, outs, operands, scalars=0, scratch=(), cost=(0, 0), whole=VMEM, fetch=(), limit=48 << 20, **more
):
    in_specs = [SMEM] * scalars + [whole] * (len(operands) - scalars)
    scratch = list(scratch)
    if fetch:
        for place in fetch:
            memory = pltpu.SMEM if place < scalars else pltpu.VMEM
            scratch.append(memory(operands[place].shape, operands[place].dtype))
            in_specs[place] = pl.BlockSpec(memory_space=pltpu.HBM)
        scratch.append(pltpu.SemaphoreType.DMA((len(fetch),)))
        kernel = functools.partial(fetching, kernel, tuple(fetch))
    return pl.pallas_call(
        kernel,
        out_shape=[jax.ShapeDtypeStruct(shape, dtype) for shape, dtype in outs],
        in_specs=in_specs,
        out_specs=[whole] * len(outs),
        scratch_shapes=scratch,
        compiler_params=pltpu.CompilerParams(vmem_limit_bytes=limit),
        cost_estimate=pl.CostEstimate(flops=cost[0], bytes_accessed=cost[1], transcendentals=0),
        name=name,
        **more,
    )(*operands)


def shards(
    density,
    margin,
    pattern_d,
    pattern_s,
    dipole,
    owner,
    centres,
    angles,
    velocity,
    angmom,
    halo_list,
    neighbours,
):
    rows, cols = density.shape
    rows_b, cols_b = pattern_d.shape
    rows_n = lax.axis_size("row")
    sub_n = lax.axis_size("sub")
    across = ("col", "sub")
    everyone = ("row", "col", "sub")
    ways = lax.axis_size("col") * sub_n
    devices = rows_n * ways
    hist_rows = rows * rows_n // LANES
    waters, listed = centres.shape[1], halo_list.shape[1]
    where = jnp.stack([lax.axis_index("row"), lax.axis_index(across)]).astype(jnp.int32)
    depth = slot_rows(rows_b, cols_b)[2]
    field_depth = -(-3 * rows_b // 8) * 8

    def swap(value, axis, count, step):
        return lax.ppermute(value, axis, [(i, i ^ step) for i in range(count)])

    def exchange(value, axis):
        return lax.all_to_all(value, axis, 0, 0, tiled=True)

    dens_all = [density] + [None] * (ways - 1)
    for step in [1] + list(range(2, ways, 2)):
        dens_all[step] = swap(density, across, ways, step)

    message, small, sites, quat, shared = call(
        functools.partial(open_kernel, ways, rows_n),
        "open",
        [
            ((devices * depth, LANES), F32),
            ((rows_n * rows, BLOCK), BF16),
            ((16, waters), F32),
            ((4, waters), F32),
            ((rows_n * 16, listed), F32),
        ],
        [where, pattern_d, pattern_s, margin, dipole, owner, centres, angles, halo_list],
        scalars=3,
        scratch=[pltpu.VMEM((hist_rows, LANES), F32)],
        cost=(10**8, 10**6),
        fetch=range(1, 9),
        limit=60 << 20,
    )
    listed_sites = exchange(shared, "row")
    received = exchange(message, everyone)
    small_all = exchange(small, "row")

    tiles = (waters + 2 * listed) // LANES
    (pair,) = call(
        functools.partial(pair_kernel, rows_n),
        "pair_forces",
        [((9, waters), F32)],
        [where, sites, listed_sites, neighbours],
        scalars=1,
        scratch=[pltpu.VMEM((9, tiles, 8, LANES), F32)],
        cost=(10**9, 10**7),
    )
    part, pot = call(
        functools.partial(project_kernel, ways, rows_n),
        "field_part",
        [((devices * field_depth, LANES), F32), ((rows_b + cols_b, LANES), F32)],
        [where, pattern_d, density, dipole, received],
        scalars=2,
        scratch=[pltpu.VMEM((8, cols), F32), pltpu.VMEM((rows, cols), BF16)],
        cost=(10**7, 10**6),
    )
    fields = exchange(part, everyone)

    for step in range(2, ways, 2):
        (dens_all[step],) = call(
            tie_kernel,
            "tie",
            [((rows, cols), BF16)],
            [dens_all[step], pair],
            whole=pl.BlockSpec(memory_space=pl.ANY),
            input_output_aliases={0: 0},
        )
        dens_all[step + 1] = swap(dens_all[step], "sub", sub_n, 1)

    (qm_out,) = call(
        functools.partial(product_kernel, ways, rows_n),
        "product",
        [((rows, cols), BF16)],
        [where, pot, received, small_all] + dens_all,
        scalars=1,
        scratch=[
            pltpu.VMEM((rows * rows_n, cols), BF16),
            pltpu.VMEM((rows, cols), BF16),
            pltpu.VMEM((rows, cols), F32),
        ],
        cost=(10**9, 10**7),
    )
    centres_new, velocity_new, angmom_new, orient_new = call(
        functools.partial(advance_kernel, ways, rows_n, rows_b),
        "advance",
        [((3, waters), F32), ((3, waters), F32), ((3, waters), F32), ((4, waters), F32)],
        [fields, owner, sites, quat, pair, centres, velocity, angmom],
        scratch=[pltpu.VMEM((16, waters), F32), pltpu.VMEM((8 * hist_rows, LANES), F32)],
        cost=(10**7, 10**6),
    )
    return (qm_out, centres_new, velocity_new, angmom_new, orient_new)


def solution(mesh):
    square = P(("groups", "row"), ("col", "sub"))
    spread = P(None, ("groups", "row", "col", "sub"))
    return jax.shard_map(
        shards,
        mesh=mesh,
        in_specs=(square,) * 4 + (P(None, ("groups", "col", "sub")),) + (spread,) * 7,
        out_specs=(square,) + (spread,) * 4,
        check_vma=False,
    )
```

time: 66.7 us -> 62.4 us (0.936)
  blocking collectives: 0 us -> 26.9 us
  waiting for transfers between devices: 25.6 us -> 9.81 us
  starting transfers between devices: 22 us -> 7.71 us
  local copies, waits for them, and re-layouts: 3.84 us -> 0.75 us
  Pallas kernels: 14.1 us -> 15.3 us
    all_to_all x0 -> x2, blocking collectives: none -> 26.9 us  [exchange(): return lax.all_to_all(value, axis, 0, 0, tiled=True)]
    ppermute x18 -> x3, waiting for transfers between devices: 24.6 us -> 0.01 us  [swap(): return lax.ppermute(value, axis, [(i, i ^ step) for i in range(count)])]
    ppermute x18 -> x3, starting transfers between devices: 18.1 us -> 0.69 us  [swap(): return lax.ppermute(value, axis, [(i, i ^ step) for i in range(count)])]
    all_to_all x0 -> x2, waiting for transfers between devices: none -> 9.8 us  [exchange(): return lax.all_to_all(value, axis, 0, 0, tiled=True)]
    all_to_all x0 -> x2, starting transfers between devices: none -> 7.02 us  [exchange(): return lax.all_to_all(value, axis, 0, 0, tiled=True)]
    ppermute x2 -> x0, starting transfers between devices: 3.86 us -> none  [ring(): lax.ppermute(value, 'row', [(i, (i + by) % rows_n) for i in range(rows_n)])]
    unnamed x28 -> x22, local copies, waits for them, and re-layouts: 3.84 us -> 0.75 us
    pallas_call x8 -> x6, Pallas kernels: 14.1 us -> 15.3 us  [call(): pl.pallas_call(kernel, out_shape=[jax.ShapeDtypeStruct(shape, dtype) for...]
  transfers between devices with their start and end apart: 20 -> 5, of which waited for: 8 -> 2; matrix products, arithmetic and copies ran while one was open for 0% -> 0% of each run, Pallas kernels for 16% -> 15%
where the time goes in v2:
time: 62.4 us; the launch traced here: 61.8 us
  blocking collectives  26.9 us (43%)
  Pallas kernels  15.3 us (25%)
  waiting for transfers between devices  9.81 us (16%)
  starting transfers between devices  7.71 us (12%)
  between operations  0.81 us (1%)
  local copies, waits for them, and re-layouts  0.75 us (1%)
    all_to_all x2, blocking collectives, exchange(): return lax.all_to_all(value, axis, 0, 0, tiled=True)  26.9 us
    pallas_call x6, Pallas kernels, call(): pl.pallas_call(kernel, out_shape=[jax.ShapeDtypeStruct(shape, dtype) for...  15.3 us
    all_to_all x2, waiting for transfers between devices, exchange(): return lax.all_to_all(value, axis, 0, 0, tiled=True)  9.8 us
    all_to_all x2, starting transfers between devices, exchange(): return lax.all_to_all(value, axis, 0, 0, tiled=True)  7.02 us
  transfers between devices with their start and end apart: 5, of which 2 were waited for; matrix products, arithmetic and copies ran while one was open for 0% of the time, Pallas kernels for 15%

profile of v2, /device:TPU:0, one launch (start us, length us, event | category | flops | bytes accessed | tf_op | source)
XLA Modules:
  0.0 61.8 jit_solution(12391914483367686464)
XLA Ops:
  0.6 0.6 pad_add_fusion.refs_0_.where
  1.2 0.0 copy-start
  1.2 3.1 %open.1 = (f32[384,128]{1,0:T(8,128)}, bf16[2048,128]{1,0:T(8,128)(2,1)}, f32[16,1024]{1,0:T(8,128)}, f32[4,1024]{1,0:T(4,128)}, f32[64,256]{1,0:T(8,128)}) custom-call(s32[2]{0:T(128)} %pad_add_fusion.refs_0_.where, s32[4,4]{1,0:T(4,128)} %pat_d.1, s32[4,4]{1,0:T(4,128)} %refs_2_.1, bf16[512,512]{1,0:T(8,128)(2,1)} %refs_3_.1, bf16[3,512]{1,0:T(4,128)(2,1)} %dip.1, ...), custom_call_target="tpu_custom_call" | custom-call | flops 100000000 | bytes 1000000 | tf_op jit(solution)/shard_map/open/pallas_call | solution.py:400
  4.3 16.4 %all_to_all.44 = f32[16,24,128]{2,1,0:T(8,128)S(1)} all-to-all(f32[16,24,128]{2,1,0:T(8,128)} %bitcast.16), channel_id=1, replica_groups=mesh['groups'=2,'row'=4,'col'=2,'sub'=2] {'row','col','sub'}, dimensions={0} | all-to-all | bytes 393216 | tf_op jit(solution)/shard_map/all_to_all | solution.py:445
  20.7 0.0 copy-start.4
  20.7 0.0 copy-start.8
  20.7 3.4 %all-to-all-start.2 = ((f32[4,16,256]{2,1,0:T(8,128)}), f32[4,16,256]{2,1,0:T(8,128)S(1)}, u32[]{:S(2)}, u32[]{:S(2)}) async-start(f32[4,16,256]{2,1,0:T(8,128)} %bitcast.6), calls=%async_computation.2 | async-start | bytes 131072 | tf_op jit(solution)/shard_map/all_to_all | solution.py:445
  24.1 0.0 copy-done
  24.1 0.0 copy-start.9
  24.1 0.1 collective-permute-start.1
  24.2 0.0 copy-done.4
  24.2 0.0 copy-done.8
  24.2 0.5 copy-done.9
  24.8 1.0 %field_part.1 = (f32[256,128]{1,0:T(8,128)S(1)}, f32[8,128]{1,0:T(8,128)S(1)}) custom-call(s32[2]{0:T(128)S(1)} %copy-done.9, s32[4,4]{1,0:T(4,128)S(1)} %copy-done.8, bf16[512,512]{1,0:T(8,128)(2,1)S(1)} %copy-done, bf16[3,512]{1,0:T(4,128)(2,1)S(1)} %copy-done.4, f32[384,128]{1,0:T(8,128)S(1)} %bitcast.10), custom_call_target="tpu_custom_call" | custom-call | flops 10000000 | bytes 1000000 | tf_op jit(solution)/shard_map/field_part/pallas_call | solution.py:400
  25.8 4.0 %all-to-all-done.2 = f32[4,16,256]{2,1,0:T(8,128)S(1)} async-done(((f32[4,16,256]{2,1,0:T(8,128)}), f32[4,16,256]{2,1,0:T(8,128)S(1)}, u32[]{:S(2)}, u32[]{:S(2)}) %all-to-all-start.2) | async-done | bytes 65568 | tf_op jit(solution)/shard_map/all_to_all | solution.py:445
  29.8 10.5 %all_to_all.45 = f32[16,16,128]{2,1,0:T(8,128)S(1)} all-to-all(f32[16,16,128]{2,1,0:T(8,128)S(1)} %bitcast.14), channel_id=1, replica_groups=mesh['groups'=2,'row'=4,'col'=2,'sub'=2] {'row','col','sub'}, dimensions={0} | all-to-all | bytes 262144 | tf_op jit(solution)/shard_map/all_to_all | solution.py:445
  40.3 0.0 copy-start.1
  40.3 0.0 copy-start.10
  40.3 3.6 %all-to-all-start.1 = ((bf16[4,512,128]{2,1,0:T(8,128)(2,1)}), bf16[4,512,128]{2,1,0:T(8,128)(2,1)S(1)}, u32[]{:S(2)}, u32[]{:S(2)}) async-start(bf16[4,512,128]{2,1,0:T(8,128)(2,1)} %bitcast.4), calls=%async_computation.1 | async-start | bytes 1048576 | tf_op jit(solution)/shard_map/all_to_all | solution.py:445
  43.9 0.1 collective-permute-start
  44.0 0.0 copy-done.1
  44.0 0.0 copy-done.10
  44.0 6.8 %pair_forces.1.second.pair = f32[9,1024]{1,0:T(8,128)S(1)} custom-call(s32[2]{0:T(128)S(1)} %copy-done.9, f32[16,1024]{1,0:T(8,128)S(1)} %copy-done.1, f32[64,256]{1,0:T(8,128)S(1)} %bitcast.15, s32[32,1024]{1,0:T(8,128)S(1)} %copy-done.10), custom_call_target="tpu_custom_call" | custom-call | flops 1000000000 | bytes 10000000 | tf_op jit(solution)/shard_map/pair_forces/pallas_call | solution.py:400
  50.9 0.0 copy-start.2
  50.9 0.0 copy-start.3
  50.9 0.0 copy-start.5
  50.9 0.0 copy-start.6
  50.9 0.0 copy-start.7
  50.9 0.0 collective-permute-done.1.first
  50.9 0.5 collective-permute-start.2
  51.5 0.1 copy-done.2
  51.6 0.0 copy-done.3
  51.6 0.0 copy-done.5
  51.6 0.0 copy-done.6
  51.6 0.0 copy-done.7
  51.6 1.2 %advance.1 = (f32[3,1024]{1,0:T(4,128)}, f32[3,1024]{1,0:T(4,128)}, f32[3,1024]{1,0:T(4,128)}, f32[4,1024]{1,0:T(4,128)}) custom-call(f32[256,128]{1,0:T(8,128)S(1)} %bitcast.13, s32[3,1024]{1,0:T(4,128)S(1)} %copy-done.2, f32[16,1024]{1,0:T(8,128)S(1)} %copy-done.1, f32[4,1024]{1,0:T(4,128)S(1)} %copy-done.7, f32[9,1024]{1,0:T(8,128)S(1)} %pair_forces.1.second.pair, ...), custom_call_target="tpu_custom_call" | custom-call | flops 10000000 | bytes 1000000 | tf_op jit(solution)/shard_map/advance/pallas_call | solution.py:400
  52.9 0.0 collective-permute-done.refs_1_
  52.9 5.8 %all-to-all-done.1 = bf16[4,512,128]{2,1,0:T(8,128)(2,1)S(1)} async-done(((bf16[4,512,128]{2,1,0:T(8,128)(2,1)}), bf16[4,512,128]{2,1,0:T(8,128)(2,1)S(1)}, u32[]{:S(2)}, u32[]{:S(2)}) %all-to-all-start.1) | async-done | bytes 524320 | tf_op jit(solution)/shard_map/all_to_all | solution.py:445
  58.7 0.0 collective-permute-done.2.refs_3_
  58.7 3.2 %product.1 = bf16[512,512]{1,0:T(8,128)(2,1)} custom-call(s32[2]{0:T(128)S(1)} %copy-done.9, f32[8,128]{1,0:T(8,128)S(1)} %get-tuple-element.17.pot, f32[384,128]{1,0:T(8,128)S(1)} %bitcast.11, bf16[2048,128]{1,0:T(8,128)(2,1)S(1)} %bitcast.12, bf16[512,512]{1,0:T(8,128)(2,1)S(1)} %copy-done, bf16[512,512]{1,0:T(8,128)(2,1)S(1)} %collective-permute-done.refs_1_, ...), custom_call_target="tpu_custom_call" | custom-call | flops 1000000000 | bytes 10000000 | tf_op jit(solution)/shard_map/product/pallas_call | solution.py:400
  (1 shorter events, 0.0 us)
Async XLA Ops:
  1.2 22.9 %copy-start = (bf16[512,512]{1,0:T(8,128)(2,1)S(1)}, bf16[512,512]{1,0:T(8,128)(2,1)}, u32[]{:S(2)}) copy-start(bf16[512,512]{1,0:T(8,128)(2,1)} %refs_0_.1) | copy-start | bytes 1572868
  20.7 3.5 %copy-start.4 = (bf16[3,512]{1,0:T(4,128)(2,1)S(1)}, bf16[3,512]{1,0:T(4,128)(2,1)}, u32[]{:S(2)}) copy-start(bf16[3,512]{1,0:T(4,128)(2,1)} %dip.1) | copy-start | bytes 9220
  20.7 3.5 %copy-start.8 = (s32[4,4]{1,0:T(4,128)S(1)}, s32[4,4]{1,0:T(4,128)}, u32[]{:S(2)}) copy-start(s32[4,4]{1,0:T(4,128)} %pat_d.1) | copy-start | bytes 196
  20.7 9.1 %all-to-all-start.2 = ((f32[4,16,256]{2,1,0:T(8,128)}), f32[4,16,256]{2,1,0:T(8,128)S(1)}, u32[]{:S(2)}, u32[]{:S(2)}) async-start(f32[4,16,256]{2,1,0:T(8,128)} %bitcast.6), calls=%async_computation.2 | async-start | bytes 131072 | tf_op jit(solution)/shard_map/all_to_all | solution.py:445
  24.1 0.7 %copy-start.9 = (s32[2]{0:T(128)S(1)}, s32[2]{0:T(128)}, u32[]{:S(2)}) copy-start(s32[2]{0:T(128)} %pad_add_fusion.refs_0_.where) | copy-start | bytes 28
  24.1 26.8 %collective-permute-start.1 = (bf16[512,512]{1,0:T(8,128)(2,1)S(1)}, bf16[512,512]{1,0:T(8,128)(2,1)S(1)}, u32[]{:S(2)}, u32[]{:S(2)}) collective-permute-start(bf16[512,512]{1,0:T(8,128)(2,1)S(1)} %copy-done), channel_id=1, source_target_pairs={{0,2},{1,3},{2,0},{3,1},{4,6},{5,7},{6,4},{7,5},{8,10},{9,11},{10,... | collective-permute-start | bytes 1572872 | tf_op jit(solution)/shard_map/ppermute | solution.py:442
  40.3 3.7 %copy-start.1 = (f32[16,1024]{1,0:T(8,128)S(1)}, f32[16,1024]{1,0:T(8,128)}, u32[]{:S(2)}) copy-start(f32[16,1024]{1,0:T(8,128)} %get-tuple-element.19.sites) | copy-start | bytes 196612
  40.3 3.7 %copy-start.10 = (s32[32,1024]{1,0:T(8,128)S(1)}, s32[32,1024]{1,0:T(8,128)}, u32[]{:S(2)}) copy-start(s32[32,1024]{1,0:T(8,128)} %neighbours.1) | copy-start | bytes 393220
  40.3 18.3 %all-to-all-start.1 = ((bf16[4,512,128]{2,1,0:T(8,128)(2,1)}), bf16[4,512,128]{2,1,0:T(8,128)(2,1)S(1)}, u32[]{:S(2)}, u32[]{:S(2)}) async-start(bf16[4,512,128]{2,1,0:T(8,128)(2,1)} %bitcast.4), calls=%async_computation.1 | async-start | bytes 1048576 | tf_op jit(solution)/shard_map/all_to_all | solution.py:445
  43.9 9.0 %collective-permute-start = (bf16[512,512]{1,0:T(8,128)(2,1)S(1)}, bf16[512,512]{1,0:T(8,128)(2,1)S(1)}, u32[]{:S(2)}, u32[]{:S(2)}) collective-permute-start(bf16[512,512]{1,0:T(8,128)(2,1)S(1)} %copy-done), channel_id=1, source_target_pairs={{0,1},{1,0},{2,3},{3,2},{4,5},{5,4},{6,7},{7,6},{8,9},{9,8},{10,11... | collective-permute-start | bytes 1572872 | tf_op jit(solution)/shard_map/ppermute | solution.py:442
  50.9 0.7 %copy-start.2 = (s32[3,1024]{1,0:T(4,128)S(1)}, s32[3,1024]{1,0:T(4,128)}, u32[]{:S(2)}) copy-start(s32[3,1024]{1,0:T(4,128)} %owner.1) | copy-start | bytes 36868
  50.9 0.7 %copy-start.3 = (f32[3,1024]{1,0:T(4,128)S(1)}, f32[3,1024]{1,0:T(4,128)}, u32[]{:S(2)}) copy-start(f32[3,1024]{1,0:T(4,128)} %centres.1) | copy-start | bytes 36868
  50.9 0.7 %copy-start.5 = (f32[3,1024]{1,0:T(4,128)S(1)}, f32[3,1024]{1,0:T(4,128)}, u32[]{:S(2)}) copy-start(f32[3,1024]{1,0:T(4,128)} %velocity.1) | copy-start | bytes 36868
  50.9 0.7 %copy-start.6 = (f32[3,1024]{1,0:T(4,128)S(1)}, f32[3,1024]{1,0:T(4,128)}, u32[]{:S(2)}) copy-start(f32[3,1024]{1,0:T(4,128)} %angmom.1) | copy-start | bytes 36868
  50.9 0.7 %copy-start.7 = (f32[4,1024]{1,0:T(4,128)S(1)}, f32[4,1024]{1,0:T(4,128)}, u32[]{:S(2)}) copy-start(f32[4,1024]{1,0:T(4,128)} %get-tuple-element.22.quat) | copy-start | bytes 49156
  50.9 7.7 %collective-permute-start.2 = (bf16[512,512]{1,0:T(8,128)(2,1)S(1)}, bf16[512,512]{1,0:T(8,128)(2,1)S(1)}, u32[]{:S(2)}, u32[]{:S(2)}) collective-permute-start(bf16[512,512]{1,0:T(8,128)(2,1)S(1)} %tie.1.refs_2_), channel_id=1, source_target_pairs={{0,1},{1,0},{2,3},{3,2},{4,5},{5,4},{6,7},{7,6},{8,9},{9,8},{10,11... | collective-permute-start | bytes 1572872 | tf_op jit(solution)/shard_map/ppermute | solution.py:442

commit v3 on v2

v3 whole, which is shorter than its diff:
```python
import functools

import jax
import jax.numpy as jnp
from jax import lax
from jax.experimental import pallas as pl
from jax.experimental.pallas import tpu as pltpu
from jax.sharding import PartitionSpec as P

BLOCK = 128
LANES = 128

CHARGE = (-0.834, 0.417, 0.417)
UNIT = 0.417
MULTIPLE = (-2.0, 1.0, 1.0)
OFFSET = ((0.0, 0.0, -0.12), (0.76, 0.0, 0.47), (-0.76, 0.0, 0.47))
COUPLE = 0.1
STEP_DT = 0.5
WATER_MASS = 1.0
INERTIA = 0.5
SOFTEN = 1.0

SHIFT = 1.0
SCALE = 65535.0 / 5.0

F32 = jnp.float32
BF16 = jnp.bfloat16

SIN_TERMS = (-1 / 6, 1 / 120, -1 / 5040, 1 / 362880, -1 / 39916800, 1 / 6227020800)
COS_TERMS = (-1 / 2, 1 / 24, -1 / 720, 1 / 40320, -1 / 3628800, 1 / 479001600, -1 / 87178291200)


def at(tile):
    return slice(tile * LANES, (tile + 1) * LANES)


def pick(table, index):
    return jnp.take_along_axis(table, index, axis=1, mode="promise_in_bounds")


def contract(left, right, dims):
    return lax.dot_general(left, right, (dims, ((), ())), preferred_element_type=F32)


def series(square, terms):
    total = jnp.full_like(square, terms[-1])
    for term in terms[-2::-1]:
        total = total * square + term
    return total * square + 1.0


def line_of(row, comp):
    return 3 * row + comp


def open_kernel(
    ways,
    hist_rows,
    where,
    pat_d,
    pat_s,
    dens,
    marg,
    dip,
    owner,
    centres,
    angles,
    halo,
    message,
    masked,
    small,
    sites,
    quat,
    listed,
):
    rows_b, cols_b = pat_d.shape
    rows, waters = dens.shape[0], owner.shape[1]
    message[...] = jnp.zeros(message.shape, F32)
    masked[rows:, :] = jnp.zeros((masked.shape[0] - rows, masked.shape[1]), BF16)
    masked[rows : rows + 3, :] = dip[...]
    lane = lax.broadcasted_iota(jnp.int32, (1, LANES), 1)
    patterns = jnp.zeros((1, LANES), F32)
    for row in range(rows_b):
        chosen = jnp.int32(0)
        lines = slice(row * BLOCK, (row + 1) * BLOCK)
        for col in range(cols_b):
            chosen = chosen + col * pat_s[row, col]
            patterns = jnp.where(lane == row * cols_b + col, pat_s[row, col].astype(F32), patterns)
            block = dens[lines, at(col)]
            masked[lines, at(col)] = jnp.where(pat_d[row, col] != 0, block, jnp.zeros_like(block))
        span = pl.ds(pl.multiple_of(chosen * BLOCK, BLOCK), BLOCK)
        block = marg[lines, span]
        small[lines, :] = block
        product = contract(dip[:, span], block, ((1,), (1,)))
        for comp in range(3):
            place = hist_rows + line_of(where[0] * rows_b + row, comp)
            message[pl.ds(place, 1), :] = product[comp : comp + 1]
    message[pl.ds(4 * hist_rows + where[0] * ways + where[1], 1), :] = patterns
    total = jnp.zeros((hist_rows, LANES), F32)
    for source in range(3):
        line = owner[source : source + 1, :]
        high = lax.broadcasted_iota(jnp.int32, (hist_rows, waters), 0) == (line >> 7)
        low = lax.broadcasted_iota(jnp.int32, (LANES, waters), 0) == (line & 127)
        total = total + contract(
            jnp.where(high, MULTIPLE[source], 0.0).astype(BF16),
            jnp.where(low, 1.0, 0.0).astype(BF16),
            ((1,), (1,)),
        )
    message[0:hist_rows, :] = total
    water_sites(centres, angles, halo, sites, quat, listed)


def water_sites(centres, angles, halo, sites, quat, listed):
    half_angle = 0.5 * angles[...]
    square = half_angle * half_angle
    sine = half_angle * series(square, SIN_TERMS)
    cosine = series(square, COS_TERMS)
    sin_r, sin_p, sin_y = sine[0:1], sine[1:2], sine[2:3]
    cos_r, cos_p, cos_y = cosine[0:1], cosine[1:2], cosine[2:3]
    comp_w = cos_r * cos_p * cos_y + sin_r * sin_p * sin_y
    comp_x = sin_r * cos_p * cos_y - cos_r * sin_p * sin_y
    comp_y = cos_r * sin_p * cos_y + sin_r * cos_p * sin_y
    comp_z = cos_r * cos_p * sin_y - sin_r * sin_p * cos_y
    for place, comp in enumerate((comp_w, comp_x, comp_y, comp_z)):
        quat[place : place + 1, :] = comp
    first = (
        1.0 - 2.0 * (comp_y * comp_y + comp_z * comp_z),
        2.0 * (comp_x * comp_y + comp_w * comp_z),
        2.0 * (comp_x * comp_z - comp_w * comp_y),
    )
    third = (
        2.0 * (comp_x * comp_z + comp_w * comp_y),
        2.0 * (comp_y * comp_z - comp_w * comp_x),
        1.0 - 2.0 * (comp_x * comp_x + comp_y * comp_y),
    )
    sites[...] = jnp.zeros(sites.shape, F32)
    for source in range(3):
        for compo in range(3):
            place = 3 * source + compo
            position = centres[compo : compo + 1, :] + third[compo] * OFFSET[source][2]
            if OFFSET[source][0] != 0.0:
                position = position + first[compo] * OFFSET[source][0]
            sites[place : place + 1, :] = position
    waters, tiles = centres.shape[1], halo.shape[1] // LANES
    used = 18 * tiles
    if used < listed.shape[0]:
        listed[used:, :] = jnp.zeros((listed.shape[0] - used, LANES), F32)
    for which in range(2):
        for tile in range(tiles):
            index = jnp.broadcast_to(halo[which : which + 1, at(tile)], (8, LANES))
            low, high = index & 127, index >> 7
            for part in range(2):
                found = jnp.zeros((8, LANES), F32)
                for source in range(waters // LANES):
                    value = pick(sites[8 * part : 8 * part + 8, at(source)], low)
                    found = jnp.where(high == source, value, found)
                for comp in range(8 * part, min(8 * part + 8, 9)):
                    place = (which * 9 + comp) * tiles + tile
                    listed[place : place + 1, :] = found[comp - 8 * part : comp - 8 * part + 1]


def merge_kernel(summed, first, second, *refs):
    more, out = refs[:-1], refs[-1]
    if summed > 0:
        out[0:summed, :] = first[0:summed, :] + second[0:summed, :]
    place = summed
    for number, ref in enumerate((first, second) + more):
        start = summed if number < 2 else 0
        count = ref.shape[0] - start
        if count > 0:
            out[place : place + count, :] = ref[start:, :]
            place = place + count


def pair_kernel(rows_n, summed, where, sites, message, neighbours, force, table):
    waters, slots = sites.shape[1], neighbours.shape[0]
    depth = (message.shape[0] - summed) // rows_n
    own_tiles = waters // LANES
    tiles = table.shape[1]
    halo_tiles = (tiles - own_tiles) // 2

    def store(tile, lines):
        fixed = [(line * SCALE + (SHIFT * SCALE + 0.5)).astype(jnp.int32) for line in lines]
        for word in range(5):
            value = fixed[2 * word]
            if word < 4:
                value = value | ((fixed[2 * word + 1] - 32768) << 16)
            table[word, tile] = jnp.broadcast_to(value, (8, LANES))

    for tile in range(own_tiles):
        store(tile, [sites[word : word + 1, at(tile)] for word in range(9)])
    for which in range(2):
        other = lax.rem(where[0] + (rows_n - 1, 1)[which], rows_n)
        start = pl.multiple_of(summed + (where[0] ^ other) * depth, 8)
        lines = message[pl.ds(start, depth), :]
        for tile in range(halo_tiles):
            places = [(which * 9 + word) * halo_tiles + tile for word in range(9)]
            store(own_tiles + which * halo_tiles + tile, [lines[place : place + 1] for place in places])

    def one_tile(tile, carry):
        span = pl.ds(pl.multiple_of(tile * LANES, LANES), LANES)
        lines = sites[:, span]
        own = []
        for word in range(9):
            line = jnp.broadcast_to(lines[word : word + 1] * SCALE + SHIFT * SCALE, (8, LANES))
            own.append((line, line - 32768.0))
        near = [jnp.zeros((8, LANES), F32) for _ in range(9)]
        far = [jnp.zeros((8, LANES), F32) for _ in range(9)]
        for pair in range(slots // 16):
            index = [neighbours[16 * pair + 8 * part : 16 * pair + 8 * part + 8, span] for part in range(2)]
            low = [value & 127 for value in index]
            high = [value >> 7 for value in index]
            found = [[None, None] for _ in range(5)]
            for source in range(tiles):
                here = [value == source for value in high]
                for word in range(5):
                    line = table[word, source]
                    for part in range(2):
                        value = pick(line, low[part])
                        found[word][part] = (
                            value if source == 0 else jnp.where(here[part], value, found[word][part])
                        )
            for part in range(2):
                places = []
                for word in range(9):
                    value = found[word // 2][part]
                    if word == 8:
                        places.append(value.astype(F32))
                    elif word % 2 == 0:
                        places.append((value & 65535).astype(F32))
                    else:
                        places.append((value >> 16).astype(F32))
                for source in range(3):
                    for target in range(3):
                        gap = []
                        for compo in range(3):
                            mine, other = 3 * source + compo, 3 * target + compo
                            gap.append(own[mine][other % 2] - places[other])
                        root = lax.rsqrt(
                            gap[0] * gap[0] + gap[1] * gap[1] + gap[2] * gap[2] + SOFTEN * SCALE * SCALE
                        )
                        weight = root * root * root
                        sums = near if target == 0 else far
                        for compo in range(3):
                            sums[3 * source + compo] = sums[3 * source + compo] + gap[compo] * weight
        for place in range(9):
            factor = CHARGE[place // 3] * UNIT * SCALE * SCALE
            total = factor * (far[place] - 2.0 * near[place])
            force[place : place + 1, span] = jnp.sum(total, axis=0, keepdims=True)
        return carry

    lax.fori_loop(0, own_tiles, one_tile, 0)


def field_kernel(ways, hist_rows, where, message, *refs):
    dens, out, lines = refs[:ways], refs[ways], refs[ways + 1]
    rows, cols = dens[0].shape[0] - 16, dens[0].shape[1]
    rows_b, cols_b = rows // BLOCK, cols // BLOCK
    result = jnp.zeros((16, rows), F32)
    lines[...] = jnp.zeros(lines.shape, F32)
    for step in range(ways):
        moments = dens[step][rows:, :].astype(F32)
        for col in range(cols_b):
            block = (where[1] ^ step) * cols_b + col
            moment = moments[0:3, at(col)]
            pot = UNIT * COUPLE * message[pl.ds(block, 1), :]
            for comp in range(3):
                product = message[pl.ds(hist_rows + line_of(block, comp), 1), :]
                lines[comp : comp + 1, at(col)] = product + pot * moment[comp : comp + 1]
            lines[3:6, at(col)] = moment
        whole = lines[...]
        first = whole.astype(BF16).astype(F32)
        both = jnp.concatenate([first, whole - first], axis=0).astype(BF16)
        result = result + contract(both, dens[step][0:rows, :], ((1,), (1,)))
    total = result[0:8] + result[8:16]
    out[...] = jnp.zeros(out.shape, F32)
    for row in range(rows_b):
        pot = UNIT * COUPLE * message[pl.ds(where[0] * rows_b + row, 1), :]
        start = line_of(row, 0)
        out[start : start + 3, :] = total[0:3, at(row)] + pot * total[3:6, at(row)]


def advance_kernel(
    rows_n,
    rows_b,
    where,
    fields,
    owner,
    sites,
    quat,
    pair,
    centres,
    velocity,
    angmom,
    centres_new,
    velocity_new,
    angmom_new,
    orient_new,
    force,
    table,
):
    waters = owner.shape[1]
    depth = fields.shape[0] // rows_n
    table[...] = jnp.zeros(table.shape, F32)
    for step in range(rows_n):
        for row in range(rows_b):
            start = step * depth + line_of(row, 0)
            place = 8 * (step * rows_b + row)
            table[place : place + 3, :] = fields[start : start + 3, :]
    for tile in range(waters // LANES):
        for source in range(3):
            index = jnp.broadcast_to(owner[source : source + 1, at(tile)], (8, LANES))
            low, high = index & 127, index >> 7
            found = jnp.zeros((8, LANES), F32)
            for step in range(rows_n):
                base = (where[0] ^ step) * rows_b
                for row in range(rows_b):
                    place = 8 * (step * rows_b + row)
                    value = pick(table[place : place + 8, :], low)
                    found = jnp.where(high == base + row, value, found)
            lines = slice(3 * source, 3 * source + 3)
            force[lines, at(tile)] = pair[lines, at(tile)] + CHARGE[source] * found[0:3]

    def cross(left, right):
        return [
            left[1] * right[2] - left[2] * right[1],
            left[2] * right[0] - left[0] * right[2],
            left[0] * right[1] - left[1] * right[0],
        ]

    def split(array):
        return [array[compo : compo + 1, :] for compo in range(3)]

    total = force[0:3, :] + force[3:6, :] + force[6:9, :]
    torque = None
    centre = split(centres)
    for source in range(3):
        lever = [sites[3 * source + compo : 3 * source + compo + 1, :] - centre[compo] for compo in range(3)]
        push = [force[3 * source + compo : 3 * source + compo + 1, :] for compo in range(3)]
        turn = cross(lever, push)
        torque = turn if torque is None else [old + new for old, new in zip(torque, turn)]
    moving = velocity[...] + STEP_DT * total / WATER_MASS
    velocity_new[...] = moving
    centres_new[...] = centres[...] + STEP_DT * moving
    spin = [angmom[compo : compo + 1, :] + STEP_DT * torque[compo] for compo in range(3)]
    for compo in range(3):
        angmom_new[compo : compo + 1, :] = spin[compo]
    omega = [value * (1.0 / INERTIA) for value in spin]
    scalar = quat[0:1, :]
    vector = [quat[compo + 1 : compo + 2, :] for compo in range(3)]
    delta = [-(omega[0] * vector[0] + omega[1] * vector[1] + omega[2] * vector[2])]
    turned = cross(omega, vector)
    delta = delta + [scalar * omega[compo] + turned[compo] for compo in range(3)]
    moved = [old + 0.5 * STEP_DT * new for old, new in zip([scalar] + vector, delta)]
    length = jnp.sqrt(moved[0] * moved[0] + moved[1] * moved[1] + moved[2] * moved[2] + moved[3] * moved[3])
    for place in range(4):
        orient_new[place : place + 1, :] = moved[place] / length


def product_kernel(ways, rows_n, hist_rows, where, message, *refs):
    dens, small = refs[:ways], refs[ways : ways + rows_n]
    out, panel, total = refs[ways + rows_n :]
    rows, cols = out.shape
    rows_b, cols_b = rows // BLOCK, cols // BLOCK
    here_row, here_col = where[0], where[1]
    for step in range(rows_n):
        other = here_row ^ step
        flags = jnp.broadcast_to(message[pl.ds(4 * hist_rows + other * ways + here_col, 1), :], (8, LANES))
        for row in range(rows_b):
            block = small[step][row * BLOCK : (row + 1) * BLOCK, :]
            for col in range(cols_b):
                flag = pick(flags, jnp.full((8, LANES), row * cols_b + col, jnp.int32))
                start = pl.multiple_of(other * rows + row * BLOCK, BLOCK)
                panel[pl.ds(start, BLOCK), at(col)] = block * flag[0:1].astype(BF16)
    ones = jnp.ones((1, LANES), F32)

    def three(value):
        first = value.astype(BF16).astype(F32)
        second = (value - first).astype(BF16).astype(F32)
        return [first, second, value - first - second]

    row_lines = [three(message[pl.ds(here_row * rows_b + row, 1), :]) for row in range(rows_b)]
    col_lines = [three(message[pl.ds(here_col * cols_b + col, 1), :]) for col in range(cols_b)]
    pad = jnp.zeros((2, LANES), F32)
    left = [jnp.concatenate(value + [ones, ones, ones, pad], axis=0).astype(BF16) for value in row_lines]
    right = [jnp.concatenate([ones, ones, ones] + value + [pad], axis=0).astype(BF16) for value in col_lines]
    for row in range(rows_b):
        for col in range(cols_b):
            spot = (slice(row * BLOCK, (row + 1) * BLOCK), at(col))
            sums = contract(left[row], right[col], ((0,), (0,)))
            total[spot] = (UNIT * COUPLE) * sums * dens[0][spot].astype(F32)
    for step in range(ways):
        start = pl.multiple_of((here_col ^ step) * cols, BLOCK)
        value = total[...] + contract(dens[step][0:rows, :], panel[pl.ds(start, cols), :], ((1,), (0,)))
        if step < ways - 1:
            total[...] = value
        else:
            out[...] = value.astype(BF16)


def tie_kernel(first, second, out):
    pass


VMEM = pl.BlockSpec(memory_space=pltpu.VMEM)
SMEM = pl.BlockSpec(memory_space=pltpu.SMEM)


def fetching(kernel, places, *refs):
    refs, semaphore = list(refs[:-1]), refs[-1]
    held = refs[len(refs) - len(places) :]
    copies = [pltpu.make_async_copy(refs[at_], held[n], semaphore.at[n]) for n, at_ in enumerate(places)]
    for copy in copies:
        copy.start()
    for copy in copies:
        copy.wait()
    for n, at_ in enumerate(places):
        refs[at_] = held[n]
    kernel(*refs[: len(refs) - len(places)])


def call(
    kernel, name, outs, operands, scalars=0, scratch=(), cost=(0, 0), whole=VMEM, fetch=(), limit=48 << 20, **more
):
    in_specs = [SMEM] * scalars + [whole] * (len(operands) - scalars)
    scratch = list(scratch)
    if fetch:
        for place in fetch:
            memory = pltpu.SMEM if place < scalars else pltpu.VMEM
            scratch.append(memory(operands[place].shape, operands[place].dtype))
            in_specs[place] = pl.BlockSpec(memory_space=pltpu.HBM)
        scratch.append(pltpu.SemaphoreType.DMA((len(fetch),)))
        kernel = functools.partial(fetching, kernel, tuple(fetch))
    return pl.pallas_call(
        kernel,
        out_shape=[jax.ShapeDtypeStruct(shape, dtype) for shape, dtype in outs],
        in_specs=in_specs,
        out_specs=[whole] * len(outs),
        scratch_shapes=scratch,
        compiler_params=pltpu.CompilerParams(vmem_limit_bytes=limit),
        cost_estimate=pl.CostEstimate(flops=cost[0], bytes_accessed=cost[1], transcendentals=0),
        name=name,
        **more,
    )(*operands)


def doublings(count):
    step = 1
    while step < count:
        yield step
        step = 2 * step


def shards(
    density,
    margin,
    pattern_d,
    pattern_s,
    dipole,
    owner,
    centres,
    angles,
    velocity,
    angmom,
    halo_list,
    neighbours,
):
    rows, cols = density.shape
    rows_b, cols_b = pattern_d.shape
    rows_n = lax.axis_size("row")
    across = ("col", "sub")
    ways = lax.axis_size("col") * lax.axis_size("sub")
    hist_rows = rows * rows_n // LANES
    waters, listed = centres.shape[1], halo_list.shape[1]
    where = jnp.stack([lax.axis_index("row"), lax.axis_index(across)]).astype(jnp.int32)
    summed = -(-(4 * hist_rows + rows_n * ways) // 8) * 8
    halo_rows = -(-18 * (listed // LANES) // 8) * 8
    field_rows = -(-3 * rows_b // 8) * 8

    def swap(value, axis, count, step):
        return lax.ppermute(value, axis, [(i, i ^ step) for i in range(count)])

    def tie(value, later):
        (value,) = call(
            tie_kernel,
            "tie",
            [(value.shape, value.dtype)],
            [value, later],
            whole=pl.BlockSpec(memory_space=pl.ANY),
            input_output_aliases={0: 0},
        )
        return value

    def merge(first, second, count, *more):
        total = count + sum(ref.shape[0] - start for ref, start in [(first, count), (second, count)])
        total = total + sum(ref.shape[0] for ref in more)
        (out,) = call(
            functools.partial(merge_kernel, count), "merge", [((total, LANES), F32)], [first, second] + list(more)
        )
        return out

    def send(value, axis, count):
        held = [value] + [None] * (count - 1)
        for step in doublings(count):
            held[step] = swap(value, axis, count, step)
        return held

    def relay(held, axis, count, later):
        for step in range(1, count):
            lowest = step & -step
            if step != lowest:
                if (step - lowest) & (step - lowest - 1) == 0:
                    held[step - lowest] = tie(held[step - lowest], later)
                held[step] = swap(held[step - lowest], axis, count, lowest)
        return held

    message, masked, small, sites, quat, halo = call(
        functools.partial(open_kernel, ways, hist_rows),
        "open",
        [
            ((summed, LANES), F32),
            ((rows + 16, cols), BF16),
            ((rows, BLOCK), BF16),
            ((16, waters), F32),
            ((4, waters), F32),
            ((halo_rows, LANES), F32),
        ],
        [where, pattern_d, pattern_s, density, margin, dipole, owner, centres, angles, halo_list],
        scalars=3,
        cost=(10**8, 10**6),
        fetch=range(1, 10),
        limit=60 << 20,
    )
    dens_all = send(masked, across, ways)
    steps = list(doublings(ways))
    for step in steps[:-1]:
        message = merge(message, swap(message, across, ways, step), summed)
    message = merge(message, swap(message, across, ways, steps[-1]), summed, halo)
    small_all = send(tie(small, message), "row", rows_n)
    for step in doublings(rows_n):
        message = merge(message, swap(message, "row", rows_n, step), summed)
    dens_all = relay(dens_all, across, ways, message)
    (field,) = call(
        functools.partial(field_kernel, ways, hist_rows),
        "field",
        [((field_rows, LANES), F32)],
        [where, message] + dens_all,
        scalars=1,
        scratch=[pltpu.VMEM((8, cols), F32)],
        cost=(10**7, 10**6),
    )
    small_all = relay(small_all, "row", rows_n, field)
    tiles = (waters + 2 * listed) // LANES
    (pair,) = call(
        functools.partial(pair_kernel, rows_n, summed),
        "pair_forces",
        [((9, waters), F32)],
        [where, sites, message, neighbours],
        scalars=1,
        scratch=[pltpu.VMEM((5, tiles, 8, LANES), jnp.int32)],
        cost=(10**9, 10**7),
    )
    for step in doublings(rows_n):
        field = merge(field, swap(field, "row", rows_n, step), 0)
    (qm_out,) = call(
        functools.partial(product_kernel, ways, rows_n, hist_rows),
        "product",
        [((rows, cols), BF16)],
        [where, message] + dens_all + small_all,
        scalars=1,
        scratch=[pltpu.VMEM((rows * rows_n, cols), BF16), pltpu.VMEM((rows, cols), F32)],
        cost=(10**9, 10**7),
    )
    centres_new, velocity_new, angmom_new, orient_new = call(
        functools.partial(advance_kernel, rows_n, rows_b),
        "advance",
        [((3, waters), F32), ((3, waters), F32), ((3, waters), F32), ((4, waters), F32)],
        [where, field, owner, sites, quat, pair, centres, velocity, angmom],
        scalars=1,
        scratch=[pltpu.VMEM((16, waters), F32), pltpu.VMEM((8 * hist_rows, LANES), F32)],
        cost=(10**7, 10**6),
    )
    return (qm_out, centres_new, velocity_new, angmom_new, orient_new)


def solution(mesh):
    square = P(("groups", "row"), ("col", "sub"))
    spread = P(None, ("groups", "row", "col", "sub"))
    return jax.shard_map(
        shards,
        mesh=mesh,
        in_specs=(square,) * 4 + (P(None, ("groups", "col", "sub")),) + (spread,) * 7,
        out_specs=(square,) + (spread,) * 4,
        check_vma=False,
    )
```

time: 62.4 us -> 59.2 us (0.949)
  blocking collectives: 26.9 us -> 0 us
  waiting for transfers between devices: 9.81 us -> 23.1 us
  starting transfers between devices: 7.71 us -> 18 us
  local copies, waits for them, and re-layouts: 0.75 us -> 2.31 us
  Pallas kernels: 15.3 us -> 14 us
    all_to_all x2 -> x0, blocking collectives: 26.9 us -> none  [exchange(): return lax.all_to_all(value, axis, 0, 0, tiled=True)]
    ppermute x3 -> x12, waiting for transfers between devices: 0.01 us -> 23.1 us  [swap(): return lax.ppermute(value, axis, [(i, i ^ step) for i in range(count)])]
    ppermute x3 -> x12, starting transfers between devices: 0.69 us -> 18 us  [swap(): return lax.ppermute(value, axis, [(i, i ^ step) for i in range(count)])]
    all_to_all x2 -> x0, waiting for transfers between devices: 9.8 us -> none  [exchange(): return lax.all_to_all(value, axis, 0, 0, tiled=True)]
    all_to_all x2 -> x0, starting transfers between devices: 7.02 us -> none  [exchange(): return lax.all_to_all(value, axis, 0, 0, tiled=True)]
    unnamed x22 -> x24, local copies, waits for them, and re-layouts: 0.75 us -> 2.31 us
    pallas_call x6 -> x14, Pallas kernels: 15.3 us -> 14 us  [call(): pl.pallas_call(kernel, out_shape=[jax.ShapeDtypeStruct(shape, dtype) for...]
  transfers between devices with their start and end apart: 5 -> 12, of which waited for: 2 -> 6; matrix products, arithmetic and copies ran while one was open for 0% -> 0% of each run, Pallas kernels for 15% -> 13%
where the time goes in v3:
time: 59.2 us; the launch traced here: 58.9 us
  waiting for transfers between devices  23.1 us (39%)
  starting transfers between devices  18 us (30%)
  Pallas kernels  14 us (24%)
  local copies, waits for them, and re-layouts  2.31 us (4%)
  between operations  0.81 us (1%)
    ppermute x12, waiting for transfers between devices, swap(): return lax.ppermute(value, axis, [(i, i ^ step) for i in range(count)])  23.1 us
    ppermute x12, starting transfers between devices, swap(): return lax.ppermute(value, axis, [(i, i ^ step) for i in range(count)])  18 us
    pallas_call x14, Pallas kernels, call(): pl.pallas_call(kernel, out_shape=[jax.ShapeDtypeStruct(shape, dtype) for...  14 us
    unnamed x24, local copies, waits for them, and re-layouts  2.31 us
  transfers between devices with their start and end apart: 12, of which 6 were waited for; matrix products, arithmetic and copies ran while one was open for 0% of the time, Pallas kernels for 13%

profile of v3, /device:TPU:0, one launch (start us, length us, event | category | flops | bytes accessed | tf_op | source)
XLA Modules:
  0.0 58.9 jit_solution(2780312846678581713)
XLA Ops:
  0.6 0.6 pad_add_fusion.refs_0_.where
  1.2 3.3 %open.1 = (f32[80,128]{1,0:T(8,128)}, bf16[528,512]{1,0:T(8,128)(2,1)}, bf16[512,128]{1,0:T(8,128)(2,1)}, f32[16,1024]{1,0:T(8,128)}, f32[4,1024]{1,0:T(4,128)}, /*index=5*/f32[40,128]{1,0:T(8,128)}) custom-call(s32[2]{0:T(128)} %pad_add_fusion.refs_0_.where, s32[4,4]{1,0:T(4,128)} %refs_1_.1, s32[4,4]{1,0:T(4,128)} %refs_2_.1, bf16[512,512]{1,0:T(8,128)(2,1)} %refs_3_.1, ...), custom_call_target="tpu_custom_call" | custom-call | flops 100000000 | bytes 1000000 | tf_op jit(solution)/shard_map/open/pallas_call | solution.py:434
  4.5 3.0 %collective-permute-start.5 = (bf16[528,512]{1,0:T(8,128)(2,1)}, bf16[528,512]{1,0:T(8,128)(2,1)S(1)}, u32[]{:S(2)}, u32[]{:S(2)}) collective-permute-start(bf16[528,512]{1,0:T(8,128)(2,1)} %get-tuple-element.17.refs_0_), channel_id=1, source_target_pairs={{0,2},{1,3},{2,0},{3,1},{4,6},{5,7},{6,4},{7,5},{8,10},{9,11},{10,... | collective-permute-start | bytes 1622024 | tf_op jit(solution)/shard_map/ppermute | solution.py:481
  7.5 0.0 collective-permute-start
  7.5 1.4 %collective-permute-done.second = f32[80,128]{1,0:T(8,128)S(1)} collective-permute-done((f32[80,128]{1,0:T(8,128)}, f32[80,128]{1,0:T(8,128)S(1)}, u32[]{:S(2)}, u32[]{:S(2)}) %collective-permute-start) | collective-permute-done | bytes 40992 | tf_op jit(solution)/shard_map/ppermute | solution.py:481
  9.0 0.0 copy-start.5
  9.0 0.8 %copy-done.5 = f32[80,128]{1,0:T(8,128)S(1)} copy-done((f32[80,128]{1,0:T(8,128)S(1)}, f32[80,128]{1,0:T(8,128)}, u32[]{:S(2)}) %copy-start.5) | copy-done | bytes 40984
  9.7 0.0 copy-start.6
  9.7 0.1 collective-permute-start.1
  9.9 11.0 %collective-permute-done.1.second = f32[80,128]{1,0:T(8,128)S(1)} collective-permute-done((f32[80,128]{1,0:T(8,128)S(1)}, f32[80,128]{1,0:T(8,128)S(1)}, u32[]{:S(2)}, u32[]{:S(2)}) %collective-permute-start.1) | collective-permute-done | bytes 40992 | tf_op jit(solution)/shard_map/ppermute | solution.py:481
  20.9 0.0 copy-done.6
  20.9 1.9 %collective-permute-start.2 = (f32[120,128]{1,0:T(8,128)S(1)}, f32[120,128]{1,0:T(8,128)S(1)}, u32[]{:S(2)}, u32[]{:S(2)}) collective-permute-start(f32[120,128]{1,0:T(8,128)S(1)} %merge.7.first.second), channel_id=1, source_target_pairs={{0,4},{4,0},{8,12},{12,8},{1,5},{5,1},{9,13},{13,9},{2,6},{6,2},{1... | collective-permute-start | bytes 184328 | tf_op jit(solution)/shard_map/ppermute | solution.py:481
  22.8 2.4 %collective-permute-done.2.second = f32[120,128]{1,0:T(8,128)S(1)} collective-permute-done((f32[120,128]{1,0:T(8,128)S(1)}, f32[120,128]{1,0:T(8,128)S(1)}, u32[]{:S(2)}, u32[]{:S(2)}) %collective-permute-start.2) | collective-permute-done | bytes 61472 | tf_op jit(solution)/shard_map/ppermute | solution.py:481
  25.2 2.9 %collective-permute-start.3 = (f32[160,128]{1,0:T(8,128)S(1)}, f32[160,128]{1,0:T(8,128)S(1)}, u32[]{:S(2)}, u32[]{:S(2)}) collective-permute-start(f32[160,128]{1,0:T(8,128)S(1)} %merge.8.first), channel_id=1, source_target_pairs={{0,8},{4,12},{8,0},{12,4},{1,9},{5,13},{9,1},{13,5},{2,10},{6,14},... | collective-permute-start | bytes 245768 | tf_op jit(solution)/shard_map/ppermute | solution.py:481
  28.1 0.0 collective-permute-start.4
  28.1 2.5 %collective-permute-done.3.second = f32[160,128]{1,0:T(8,128)S(1)} collective-permute-done((f32[160,128]{1,0:T(8,128)S(1)}, f32[160,128]{1,0:T(8,128)S(1)}, u32[]{:S(2)}, u32[]{:S(2)}) %collective-permute-start.3) | collective-permute-done | bytes 81952 | tf_op jit(solution)/shard_map/ppermute | solution.py:481
  30.6 0.0 copy-start.1
  30.6 0.0 copy-start
  30.6 0.0 collective-permute-done.5.first
  30.7 0.1 collective-permute-start.6
  30.7 0.8 %copy-done.1 = bf16[512,128]{1,0:T(8,128)(2,1)S(1)} copy-done((bf16[512,128]{1,0:T(8,128)(2,1)S(1)}, bf16[512,128]{1,0:T(8,128)(2,1)}, u32[]{:S(2)}) %copy-start.1) | copy-done | bytes 131096
  31.5 0.0 copy-start.10
  31.5 2.9 %collective-permute-start.8 = (bf16[512,128]{1,0:T(8,128)(2,1)S(1)}, bf16[512,128]{1,0:T(8,128)(2,1)S(1)}, u32[]{:S(2)}, u32[]{:S(2)}) collective-permute-start(bf16[512,128]{1,0:T(8,128)(2,1)S(1)} %tie.4.refs_4_), channel_id=1, source_target_pairs={{0,8},{4,12},{8,0},{12,4},{1,9},{5,13},{9,1},{13,5},{2,10},{6,14},... | collective-permute-start | bytes 393224 | tf_op jit(solution)/shard_map/ppermute | solution.py:481
  34.5 2.3 %collective-permute-start.7 = (bf16[512,128]{1,0:T(8,128)(2,1)S(1)}, bf16[512,128]{1,0:T(8,128)(2,1)S(1)}, u32[]{:S(2)}, u32[]{:S(2)}) collective-permute-start(bf16[512,128]{1,0:T(8,128)(2,1)S(1)} %tie.4.refs_4_), channel_id=1, source_target_pairs={{0,4},{4,0},{8,12},{12,8},{1,5},{5,1},{9,13},{13,9},{2,6},{6,2},{1... | collective-permute-start | bytes 393224 | tf_op jit(solution)/shard_map/ppermute | solution.py:481
  36.7 0.0 collective-permute-done.4.refs_1_
  36.7 0.0 collective-permute-done.6.refs_3_
  36.7 0.0 copy-done
  36.7 0.0 copy-done.10
  36.7 1.2 %field.1.second.first = f32[16,128]{1,0:T(8,128)S(1)} custom-call(s32[2]{0:T(128)S(1)} %copy-done.10, f32[240,128]{1,0:T(8,128)S(1)} %merge.9.second.message, bf16[528,512]{1,0:T(8,128)(2,1)S(1)} %copy-done, bf16[528,512]{1,0:T(8,128)(2,1)S(1)} %collective-permute-done.4.refs_1_, bf16[528,512]{1,0:T(8,128)(2,1)S(1)} %tie.3.refs_2_, ...), custom_call_target="tpu_custom_call" | custom-call | flops 10000000 | bytes 1000000 | tf_op jit(solution)/shard_map/field/pallas_call | solution.py:434
  37.9 0.0 copy-start.4
  37.9 0.0 copy-start.11
  38.0 2.8 %collective-permute-done.8.first = bf16[512,128]{1,0:T(8,128)(2,1)S(1)} collective-permute-done((bf16[512,128]{1,0:T(8,128)(2,1)S(1)}, bf16[512,128]{1,0:T(8,128)(2,1)S(1)}, u32[]{:S(2)}, u32[]{:S(2)}) %collective-permute-start.8) | collective-permute-done | bytes 131104 | tf_op jit(solution)/shard_map/ppermute | solution.py:481
  40.7 0.6 %collective-permute-start.9 = (bf16[512,128]{1,0:T(8,128)(2,1)S(1)}, bf16[512,128]{1,0:T(8,128)(2,1)S(1)}, u32[]{:S(2)}, u32[]{:S(2)}) collective-permute-start(bf16[512,128]{1,0:T(8,128)(2,1)S(1)} %tie.5.refs_6_), channel_id=1, source_target_pairs={{0,4},{4,0},{8,12},{12,8},{1,5},{5,1},{9,13},{13,9},{2,6},{6,2},{1... | collective-permute-start | bytes 393224 | tf_op jit(solution)/shard_map/ppermute | solution.py:481
  41.4 1.4 %collective-permute-start.10 = (f32[16,128]{1,0:T(8,128)S(1)}, f32[16,128]{1,0:T(8,128)S(1)}, u32[]{:S(2)}, u32[]{:S(2)}) collective-permute-start(f32[16,128]{1,0:T(8,128)S(1)} %field.1.second.first), channel_id=1, source_target_pairs={{0,4},{4,0},{8,12},{12,8},{1,5},{5,1},{9,13},{13,9},{2,6},{6,2},{1... | collective-permute-start | bytes 24584 | tf_op jit(solution)/shard_map/ppermute | solution.py:481
  42.8 3.0 %collective-permute-done.10.second = f32[16,128]{1,0:T(8,128)S(1)} collective-permute-done((f32[16,128]{1,0:T(8,128)S(1)}, f32[16,128]{1,0:T(8,128)S(1)}, u32[]{:S(2)}, u32[]{:S(2)}) %collective-permute-start.10) | collective-permute-done | bytes 8224 | tf_op jit(solution)/shard_map/ppermute | solution.py:481
  45.8 2.8 %collective-permute-start.11 = (f32[32,128]{1,0:T(8,128)S(1)}, f32[32,128]{1,0:T(8,128)S(1)}, u32[]{:S(2)}, u32[]{:S(2)}) collective-permute-start(f32[32,128]{1,0:T(8,128)S(1)} %merge.10.first), channel_id=1, source_target_pairs={{0,8},{4,12},{8,0},{12,4},{1,9},{5,13},{9,1},{13,5},{2,10},{6,14},... | collective-permute-start | bytes 49160 | tf_op jit(solution)/shard_map/ppermute | solution.py:481
  48.6 0.0 copy-done.4
  48.6 0.0 copy-done.11
  48.6 0.0 copy-start.9
  48.6 4.5 %pair_forces.1.pair = f32[9,1024]{1,0:T(8,128)S(1)} custom-call(s32[2]{0:T(128)S(1)} %copy-done.10, f32[16,1024]{1,0:T(8,128)S(1)} %copy-done.4, f32[240,128]{1,0:T(8,128)S(1)} %merge.9.second.message, s32[32,1024]{1,0:T(8,128)S(1)} %copy-done.11), custom_call_target="tpu_custom_call" | custom-call | flops 1000000000 | bytes 10000000 | tf_op jit(solution)/shard_map/pair_forces/pallas_call | solution.py:434
  53.1 0.0 copy-start.2
  53.1 0.0 copy-start.3
  53.1 0.0 copy-start.7
  53.2 0.0 copy-start.8
  53.2 0.0 collective-permute-done.11.second
  53.2 0.0 copy-done.9
  53.2 0.6 %copy-done.2 = s32[3,1024]{1,0:T(4,128)S(1)} copy-done((s32[3,1024]{1,0:T(4,128)S(1)}, s32[3,1024]{1,0:T(4,128)}, u32[]{:S(2)}) %copy-start.2) | copy-done | bytes 12312
  53.8 0.0 copy-done.3
  53.9 0.0 copy-done.7
  53.9 0.0 copy-done.8
  53.9 1.8 %advance.1 = (f32[3,1024]{1,0:T(4,128)}, f32[3,1024]{1,0:T(4,128)}, f32[3,1024]{1,0:T(4,128)}, f32[4,1024]{1,0:T(4,128)}) custom-call(s32[2]{0:T(128)S(1)} %copy-done.10, f32[64,128]{1,0:T(8,128)S(1)} %merge.11.fields, s32[3,1024]{1,0:T(4,128)S(1)} %copy-done.2, f32[16,1024]{1,0:T(8,128)S(1)} %copy-done.4, f32[4,1024]{1,0:T(4,128)S(1)} %copy-done.9, ...), custom_call_target="tpu_custom_call" | custom-call | flops 10000000 | bytes 1000000 | tf_op jit(solution)/shard_map/advance/pallas_call | solution.py:434
  55.7 0.0 collective-permute-done.7.refs_5_
  55.7 0.0 collective-permute-done.9.refs_7_
  55.7 3.2 %product.1 = bf16[512,512]{1,0:T(8,128)(2,1)} custom-call(s32[2]{0:T(128)S(1)} %copy-done.10, f32[240,128]{1,0:T(8,128)S(1)} %merge.9.second.message, bf16[528,512]{1,0:T(8,128)(2,1)S(1)} %copy-done, bf16[528,512]{1,0:T(8,128)(2,1)S(1)} %collective-permute-done.4.refs_1_, bf16[528,512]{1,0:T(8,128)(2,1)S(1)} %tie.3.refs_2_, ...), custom_call_target="tpu_custom_call" | custom-call | flops 1000000000 | bytes 10000000 | tf_op jit(solution)/shard_map/product/pallas_call | solution.py:434
  (9 shorter events, 0.0 us)
Async XLA Ops:
  4.5 26.1 %collective-permute-start.5 = (bf16[528,512]{1,0:T(8,128)(2,1)}, bf16[528,512]{1,0:T(8,128)(2,1)S(1)}, u32[]{:S(2)}, u32[]{:S(2)}) collective-permute-start(bf16[528,512]{1,0:T(8,128)(2,1)} %get-tuple-element.17.refs_0_), channel_id=1, source_target_pairs={{0,2},{1,3},{2,0},{3,1},{4,6},{5,7},{6,4},{7,5},{8,10},{9,11},{10,... | collective-permute-start | bytes 1622024 | tf_op jit(solution)/shard_map/ppermute | solution.py:481
  7.5 1.4 %collective-permute-start = (f32[80,128]{1,0:T(8,128)}, f32[80,128]{1,0:T(8,128)S(1)}, u32[]{:S(2)}, u32[]{:S(2)}) collective-permute-start(f32[80,128]{1,0:T(8,128)} %get-tuple-element.15.first), channel_id=1, source_target_pairs={{0,1},{1,0},{2,3},{3,2},{4,5},{5,4},{6,7},{7,6},{8,9},{9,8},{10,11... | collective-permute-start | bytes 122888 | tf_op jit(solution)/shard_map/ppermute | solution.py:481
  9.0 0.8 %copy-start.5 = (f32[80,128]{1,0:T(8,128)S(1)}, f32[80,128]{1,0:T(8,128)}, u32[]{:S(2)}) copy-start(f32[80,128]{1,0:T(8,128)} %get-tuple-element.15.first) | copy-start | bytes 122884
  9.7 11.2 %copy-start.6 = (f32[40,128]{1,0:T(8,128)S(1)}, f32[40,128]{1,0:T(8,128)}, u32[]{:S(2)}) copy-start(f32[40,128]{1,0:T(8,128)} %get-tuple-element.16.refs_0_) | copy-start | bytes 61444
  9.7 11.1 %collective-permute-start.1 = (f32[80,128]{1,0:T(8,128)S(1)}, f32[80,128]{1,0:T(8,128)S(1)}, u32[]{:S(2)}, u32[]{:S(2)}) collective-permute-start(f32[80,128]{1,0:T(8,128)S(1)} %merge.6.first), channel_id=1, source_target_pairs={{0,2},{1,3},{2,0},{3,1},{4,6},{5,7},{6,4},{7,5},{8,10},{9,11},{10,... | collective-permute-start | bytes 122888 | tf_op jit(solution)/shard_map/ppermute | solution.py:481
  20.9 4.3 %collective-permute-start.2 = (f32[120,128]{1,0:T(8,128)S(1)}, f32[120,128]{1,0:T(8,128)S(1)}, u32[]{:S(2)}, u32[]{:S(2)}) collective-permute-start(f32[120,128]{1,0:T(8,128)S(1)} %merge.7.first.second), channel_id=1, source_target_pairs={{0,4},{4,0},{8,12},{12,8},{1,5},{5,1},{9,13},{13,9},{2,6},{6,2},{1... | collective-permute-start | bytes 184328 | tf_op jit(solution)/shard_map/ppermute | solution.py:481
  25.2 5.4 %collective-permute-start.3 = (f32[160,128]{1,0:T(8,128)S(1)}, f32[160,128]{1,0:T(8,128)S(1)}, u32[]{:S(2)}, u32[]{:S(2)}) collective-permute-start(f32[160,128]{1,0:T(8,128)S(1)} %merge.8.first), channel_id=1, source_target_pairs={{0,8},{4,12},{8,0},{12,4},{1,9},{5,13},{9,1},{13,5},{2,10},{6,14},... | collective-permute-start | bytes 245768 | tf_op jit(solution)/shard_map/ppermute | solution.py:481
  28.1 8.6 %collective-permute-start.4 = (bf16[528,512]{1,0:T(8,128)(2,1)}, bf16[528,512]{1,0:T(8,128)(2,1)S(1)}, u32[]{:S(2)}, u32[]{:S(2)}) collective-permute-start(bf16[528,512]{1,0:T(8,128)(2,1)} %get-tuple-element.17.refs_0_), channel_id=1, source_target_pairs={{0,1},{1,0},{2,3},{3,2},{4,5},{5,4},{6,7},{7,6},{8,9},{9,8},{10,11... | collective-permute-start | bytes 1622024 | tf_op jit(solution)/shard_map/ppermute | solution.py:481
  30.6 0.9 %copy-start.1 = (bf16[512,128]{1,0:T(8,128)(2,1)S(1)}, bf16[512,128]{1,0:T(8,128)(2,1)}, u32[]{:S(2)}) copy-start(bf16[512,128]{1,0:T(8,128)(2,1)} %get-tuple-element.18.first) | copy-start | bytes 393220
  30.6 6.1 %copy-start = (bf16[528,512]{1,0:T(8,128)(2,1)S(1)}, bf16[528,512]{1,0:T(8,128)(2,1)}, u32[]{:S(2)}) copy-start(bf16[528,512]{1,0:T(8,128)(2,1)} %get-tuple-element.17.refs_0_) | copy-start | bytes 1622020
  30.7 6.1 %collective-permute-start.6 = (bf16[528,512]{1,0:T(8,128)(2,1)S(1)}, bf16[528,512]{1,0:T(8,128)(2,1)S(1)}, u32[]{:S(2)}, u32[]{:S(2)}) collective-permute-start(bf16[528,512]{1,0:T(8,128)(2,1)S(1)} %tie.3.refs_2_), channel_id=1, source_target_pairs={{0,1},{1,0},{2,3},{3,2},{4,5},{5,4},{6,7},{7,6},{8,9},{9,8},{10,11... | collective-permute-start | bytes 1622024 | tf_op jit(solution)/shard_map/ppermute | solution.py:481
  31.5 5.2 %copy-start.10 = (s32[2]{0:T(128)S(1)}, s32[2]{0:T(128)}, u32[]{:S(2)}) copy-start(s32[2]{0:T(128)} %pad_add_fusion.refs_0_.where) | copy-start | bytes 28
  31.5 9.2 %collective-permute-start.8 = (bf16[512,128]{1,0:T(8,128)(2,1)S(1)}, bf16[512,128]{1,0:T(8,128)(2,1)S(1)}, u32[]{:S(2)}, u32[]{:S(2)}) collective-permute-start(bf16[512,128]{1,0:T(8,128)(2,1)S(1)} %tie.4.refs_4_), channel_id=1, source_target_pairs={{0,8},{4,12},{8,0},{12,4},{1,9},{5,13},{9,1},{13,5},{2,10},{6,14},... | collective-permute-start | bytes 393224 | tf_op jit(solution)/shard_map/ppermute | solution.py:481
  34.5 21.2 %collective-permute-start.7 = (bf16[512,128]{1,0:T(8,128)(2,1)S(1)}, bf16[512,128]{1,0:T(8,128)(2,1)S(1)}, u32[]{:S(2)}, u32[]{:S(2)}) collective-permute-start(bf16[512,128]{1,0:T(8,128)(2,1)S(1)} %tie.4.refs_4_), channel_id=1, source_target_pairs={{0,4},{4,0},{8,12},{12,8},{1,5},{5,1},{9,13},{13,9},{2,6},{6,2},{1... | collective-permute-start | bytes 393224 | tf_op jit(solution)/shard_map/ppermute | solution.py:481
  37.9 10.7 %copy-start.4 = (f32[16,1024]{1,0:T(8,128)S(1)}, f32[16,1024]{1,0:T(8,128)}, u32[]{:S(2)}) copy-start(f32[16,1024]{1,0:T(8,128)} %get-tuple-element.19.sites) | copy-start | bytes 196612
  37.9 10.7 %copy-start.11 = (s32[32,1024]{1,0:T(8,128)S(1)}, s32[32,1024]{1,0:T(8,128)}, u32[]{:S(2)}) copy-start(s32[32,1024]{1,0:T(8,128)} %neighbours.1) | copy-start | bytes 393220
  40.7 14.9 %collective-permute-start.9 = (bf16[512,128]{1,0:T(8,128)(2,1)S(1)}, bf16[512,128]{1,0:T(8,128)(2,1)S(1)}, u32[]{:S(2)}, u32[]{:S(2)}) collective-permute-start(bf16[512,128]{1,0:T(8,128)(2,1)S(1)} %tie.5.refs_6_), channel_id=1, source_target_pairs={{0,4},{4,0},{8,12},{12,8},{1,5},{5,1},{9,13},{13,9},{2,6},{6,2},{1... | collective-permute-start | bytes 393224 | tf_op jit(solution)/shard_map/ppermute | solution.py:481
  41.4 4.4 %collective-permute-start.10 = (f32[16,128]{1,0:T(8,128)S(1)}, f32[16,128]{1,0:T(8,128)S(1)}, u32[]{:S(2)}, u32[]{:S(2)}) collective-permute-start(f32[16,128]{1,0:T(8,128)S(1)} %field.1.second.first), channel_id=1, source_target_pairs={{0,4},{4,0},{8,12},{12,8},{1,5},{5,1},{9,13},{13,9},{2,6},{6,2},{1... | collective-permute-start | bytes 24584 | tf_op jit(solution)/shard_map/ppermute | solution.py:481
  45.8 7.4 %collective-permute-start.11 = (f32[32,128]{1,0:T(8,128)S(1)}, f32[32,128]{1,0:T(8,128)S(1)}, u32[]{:S(2)}, u32[]{:S(2)}) collective-permute-start(f32[32,128]{1,0:T(8,128)S(1)} %merge.10.first), channel_id=1, source_target_pairs={{0,8},{4,12},{8,0},{12,4},{1,9},{5,13},{9,1},{13,5},{2,10},{6,14},... | collective-permute-start | bytes 49160 | tf_op jit(solution)/shard_map/ppermute | solution.py:481
  48.6 4.6 %copy-start.9 = (f32[4,1024]{1,0:T(4,128)S(1)}, f32[4,1024]{1,0:T(4,128)}, u32[]{:S(2)}) copy-start(f32[4,1024]{1,0:T(4,128)} %get-tuple-element.20.quat) | copy-start | bytes 49156
  53.1 0.7 %copy-start.2 = (s32[3,1024]{1,0:T(4,128)S(1)}, s32[3,1024]{1,0:T(4,128)}, u32[]{:S(2)}) copy-start(s32[3,1024]{1,0:T(4,128)} %owner.1) | copy-start | bytes 36868
  53.1 0.7 %copy-start.3 = (f32[3,1024]{1,0:T(4,128)S(1)}, f32[3,1024]{1,0:T(4,128)}, u32[]{:S(2)}) copy-start(f32[3,1024]{1,0:T(4,128)} %centres.1) | copy-start | bytes 36868
  53.1 0.7 %copy-start.7 = (f32[3,1024]{1,0:T(4,128)S(1)}, f32[3,1024]{1,0:T(4,128)}, u32[]{:S(2)}) copy-start(f32[3,1024]{1,0:T(4,128)} %velocity.1) | copy-start | bytes 36868
  53.2 0.7 %copy-start.8 = (f32[3,1024]{1,0:T(4,128)S(1)}, f32[3,1024]{1,0:T(4,128)}, u32[]{:S(2)}) copy-start(f32[3,1024]{1,0:T(4,128)} %angmom.1) | copy-start | bytes 36868
